TPU v7x, 32 devices: a whole 2x2x4 slice. The times are simulated.
32 devices in a mesh: rep: 8 (over y, x, core), mdl: 4 (over z).
Axes of the slice: x: 2, y: 2, z: 4, core: 2. Of those that a mesh axis runs over, the one named last changes fastest.
Arguments:
- token_ids: int32 [8, 512], P('rep'), may hold values from 0 to 383
- lengths: int32 [8], P('rep'), may hold values from 64 to 512
- embedding: bfloat16 [384, 2560], P(None, 'mdl'), may hold values from -105 to 105
- norm_gain: bfloat16 [2560], P('mdl'), may hold values from 0.099609375 to 1.8984375
- scores: bfloat16 [8, 32, 512, 512], P('rep', 'mdl'), may hold values from -12 to 300
- cotangent: bfloat16 [8, 512, 2560], P('rep', None, 'mdl'), may hold values from -4 to 4
- w_value: bfloat16 [2560, 2048], P(None, 'mdl'), may hold values from -0.125 to 0.125
- w_out: bfloat16 [2048, 2560], P('mdl'), may hold values from -0.125 to 0.125
- err_value: bfloat16 [8, 2560, 2048], P('rep', None, 'mdl'), may hold values from -6 to 6
- err_out: bfloat16 [8, 2048, 2560], P('rep', 'mdl'), may hold values from -6 to 6
- q_value: float32 [2048, 64], P('mdl'), may hold values from -6 to 6
- q_out: float32 [2048, 64], P('mdl'), may hold values from -6 to 6
Outputs:
- update_value: bfloat16 [2560, 2048], P(None, 'mdl')
- update_out: bfloat16 [2048, 2560], P('mdl')
- new_err_value: bfloat16 [8, 2560, 2048], P('rep', None, 'mdl')
- new_err_out: bfloat16 [8, 2048, 2560], P('rep', 'mdl')
- new_q_value: float32 [2048, 64], P('mdl')
- new_q_out: float32 [2048, 64], P('mdl')
All inputs are finite; a program needn't handle non-finite values.
Results may differ from a plain program's by a relative error of at most 0.02.
Values may be sent and summed in bfloat16 or wider, within the bound.
A program may use at most 128 MiB of HBM per device.

v0:
```python
import jax
import jax.numpy as jnp
from jax import lax
from jax.sharding import PartitionSpec as P

HIGH = lax.Precision.HIGHEST


def orthonormal_rows(rows_part, gram):
    lower = jnp.linalg.cholesky(gram)
    return jax.scipy.linalg.solve_triangular(lower, rows_part.T, lower=True).T


def self_gram(matrix):
    return lax.dot_general(matrix, matrix, (((0,), (0,)), ((), ())), precision=HIGH)


def shards(
    token_ids,
    lengths,
    embedding,
    norm_gain,
    scores,
    cotangent,
    w_value,
    w_out,
    err_value,
    err_out,
    q_value,
    q_out,
):
    samples, seq = token_ids.shape
    vocab = embedding.shape[0]
    rows = samples * seq
    flat_ids = token_ids.reshape(rows)
    onehot = (flat_ids[:, None] == jnp.arange(vocab, dtype=jnp.int32)[None, :]).astype(jnp.bfloat16)
    x_local = jnp.dot(onehot, embedding, preferred_element_type=jnp.float32)
    squares = jnp.sum(x_local * x_local, axis=1)
    totals = lax.psum(squares, "mdl")
    width = x_local.shape[1] * lax.axis_size("mdl")
    scale = lax.rsqrt(totals / width + 1e-06)
    normed_local = (x_local * scale[:, None] * norm_gain.astype(jnp.float32)[None, :]).astype(
        jnp.bfloat16
    )
    normed = lax.all_gather(normed_local, "mdl", axis=1, tiled=True)
    dy_whole = lax.all_gather(cotangent, "mdl", axis=2, tiled=True)
    width_full = dy_whole.shape[2]
    live = jnp.arange(seq, dtype=jnp.int32)[None, :] < lengths[:, None]
    dy_rows = jnp.where(live[..., None], dy_whole, jnp.zeros_like(dy_whole)).reshape(
        rows, width_full
    )
    heads_local = scores.shape[1]
    inner_local = w_value.shape[1]
    head_size = inner_local // heads_local
    values = jnp.dot(normed, w_value, preferred_element_type=jnp.float32).astype(jnp.bfloat16)
    logits = jnp.where(live[:, None, None, :], scores.astype(jnp.float32), jnp.float32(-1e30))
    top = jnp.max(logits, axis=-1, keepdims=True)
    expo = jnp.exp(logits - top)
    weights = (expo / jnp.sum(expo, axis=-1, keepdims=True)).astype(jnp.bfloat16)
    values4 = values.reshape(samples, seq, heads_local, head_size)
    context = (
        jnp.einsum("shqk,skhd->sqhd", weights, values4, preferred_element_type=jnp.float32)
        .astype(jnp.bfloat16)
        .reshape(rows, inner_local)
    )
    grad_out = lax.dot_general(
        context, dy_rows, (((0,), (0,)), ((), ())), preferred_element_type=jnp.float32
    )
    dcontext = lax.dot_general(
        dy_rows, w_out, (((1,), (1,)), ((), ())), preferred_element_type=jnp.float32
    ).astype(jnp.bfloat16)
    dctx4 = dcontext.reshape(samples, seq, heads_local, head_size)
    dvalues = (
        jnp.einsum("shqk,sqhd->skhd", weights, dctx4, preferred_element_type=jnp.float32)
        .astype(jnp.bfloat16)
        .reshape(rows, inner_local)
    )
    grad_value = lax.dot_general(
        normed, dvalues, (((0,), (0,)), ((), ())), preferred_element_type=jnp.float32
    )
    mem_value = grad_value + err_value[0].astype(jnp.float32)
    mem_out = grad_out + err_out[0].astype(jnp.float32)
    p_value = jnp.dot(mem_value, q_value, precision=HIGH)
    p_out = lax.dot_general(mem_out, q_out, (((0,), (0,)), ((), ())), precision=HIGH)
    sum_value, sum_out = lax.psum((p_value, p_out), ("rep", "mdl"))
    phat_value = orthonormal_rows(sum_value, self_gram(sum_value))
    phat_out = orthonormal_rows(sum_out, self_gram(sum_out))
    term_value = lax.dot_general(mem_value, phat_value, (((0,), (0,)), ((), ())), precision=HIGH)
    term_out = jnp.dot(mem_out, phat_out, precision=HIGH)
    total_value, total_out = lax.psum((term_value, term_out), "rep")
    replicas = lax.axis_size("rep")
    new_q_value = total_value / replicas
    new_q_out = total_out / replicas
    full_value = lax.dot_general(phat_value, new_q_value, (((1,), (1,)), ((), ())), precision=HIGH)
    full_out = lax.dot_general(new_q_out, phat_out, (((1,), (1,)), ((), ())), precision=HIGH)
    new_err_value = (mem_value - full_value).astype(jnp.bfloat16)[None]
    new_err_out = (mem_out - full_out).astype(jnp.bfloat16)[None]
    return (
        full_value.astype(jnp.bfloat16),
        full_out.astype(jnp.bfloat16),
        new_err_value,
        new_err_out,
        new_q_value,
        new_q_out,
    )


def solution(mesh):
    return jax.shard_map(
        shards,
        mesh=mesh,
        in_specs=(
            P("rep", None),
            P("rep"),
            P(None, "mdl"),
            P("mdl"),
            P("rep", "mdl", None, None),
            P("rep", None, "mdl"),
            P(None, "mdl"),
            P("mdl", None),
            P("rep", None, "mdl"),
            P("rep", "mdl", None),
            P("mdl", None),
            P("mdl", None),
        ),
        out_specs=(
            P(None, "mdl"),
            P("mdl", None),
            P("rep", None, "mdl"),
            P("rep", "mdl", None),
            P("mdl", None),
            P("mdl", None),
        ),
        check_vma=False,
    )
```

profile of v0, /device:TPU:0, one launch (start us, length us, event | category | flops | bytes accessed | tf_op | source)
XLA Modules:
  0.0 412.2 jit_solution(16765810818400986495)
XLA Ops:
  8.1 2.7 multiply_reduce_fusion
  10.8 13.4 %psum.35 = f32[512]{0:T(512)S(1)} all-reduce(f32[512]{0:T(512)S(1)} %get-tuple-element.16), channel_id=1, replica_groups=mesh['rep'=8,'mdl'=4] {'mdl'}, use_global_device_ids=true, to_apply=%region_1.0 | all-reduce | flops 512 | bytes 4096 | tf_op jit(solution)/shard_map/psum | solution.py:39
  24.2 2.3 multiply_convert_fusion
  28.2 3.3 fusion
  31.4 2.1 fusion.1
  33.5 3.6 fusion.2
  37.1 42.5 %all-gather.3.cloned.1.call-done = bf16[512,2560]{1,0:T(8,128)(2,1)} async-done(((bf16[512,640]{1,0:T(8,128)(2,1)}), bf16[512,2560]{1,0:T(8,128)(2,1)}) %all-gather.3.cloned.1.call-update) | async-done | bytes 2621456 | tf_op jit(solution)/shard_map/all_gather | solution.py:45
  79.6 3.5 convolution_convert_fusion.2
  84.5 50.1 %all-gather.5.cloned.1.call-done = bf16[1,512,2560]{2,1,0:T(8,128)(2,1)} async-done(((bf16[1,512,640]{2,1,0:T(8,128)(2,1)}), bf16[1,512,2560]{2,1,0:T(8,128)(2,1)}) %all-gather.5.cloned.1.call-update) | async-done | bytes 2621456 | tf_op jit(solution)/shard_map/all_gather | solution.py:46
  134.6 4.3 %fusion.8 = bf16[512,512]{0,1:T(8,128)(2,1)S(1)} fusion(bf16[512,2560]{1,0:T(8,128)(2,1)} %param.22, bf16[1,512,2560]{2,1,0:T(8,128)(2,1)} %all-gather.5.cloned.1.call-done, pred[512]{0:T(512)(128)(4,1)S(1)} %iota_compare_fusion.4), kind=kOutput, calls=%fused_computation.20 | convolution fusion | flops 1343750144 | bytes 5767680 | tf_op jit(solution)/shard_map/dot_general | solution.py:69
  143.1 4.4 %fusion.28 = f32[2560,64]{0,1:T(8,128)} fusion(f32[512,2560]{1,0:T(8,128)S(1)} %convert_add_fusion, f32[512,64]{0,1:T(8,128)S(1)} %copy-done.13), kind=kOutput, calls=%fused_computation.54 | convolution fusion | flops 1006632960 | bytes 6029312 | tf_op jit(solution)/shard_map/dot_general | solution.py:84
  149.1 2.3 copy-done.1
  151.5 6.3 %fusion.25 = f32[2560,64]{0,1:T(8,128)} fusion(f32[2560,512]{1,0:T(8,128)S(1)} %convert_add_fusion.1, f32[512,64]{0,1:T(8,128)S(1)} %copy-done.14), kind=kOutput, calls=%fused_computation.51 | convolution fusion | flops 1006632960 | bytes 6029312 | tf_op jit(solution)/shard_map/dot_general | solution.py:83
  157.8 130.3 %all-reduce.5.cloned.1.call-done = (f32[2560,64]{0,1:T(8,128)}, f32[2560,64]{0,1:T(8,128)}) async-done(((f32[2560,64]{0,1:T(8,128)}, f32[2560,64]{0,1:T(8,128)}), (f32[2560,64]{0,1:T(8,128)}, f32[2560,64]{0,1:T(8,128)})) %all-reduce.5.cloned.1.call-update) | async-done | bytes 1310736 | tf_op jit(solution)/shard_map/psum | solution.py:85
  288.1 2.0 fusion.26
  292.1 5.8 %cholesky.55 = f32[64,64]{1,0:T(8,128)S(1)} custom-call(f32[64,64]{1,0:T(8,128)S(1)} %fusion.20), custom_call_target="Cholesky" | custom-call | tf_op jit(solution)/shard_map/jit(cholesky)/cholesky | solution.py:10
  299.3 4.9 %custom-call.7 = f32[1,64,64]{1,2,0:T(8,128)S(1)} custom-call(f32[1,64,64]{2,1,0:T(8,128)S(1)} %fusion.18), custom_call_target="InvertDiagBlocksLowerTriangular" | custom-call | tf_op jit(solution)/shard_map/jit(_solve_triangular)/triangular_solve | solution.py:11
  306.2 5.8 %cholesky.44 = f32[64,64]{1,0:T(8,128)S(1)} custom-call(f32[64,64]{1,0:T(8,128)S(1)} %fusion.22), custom_call_target="Cholesky" | custom-call | tf_op jit(solution)/shard_map/jit(cholesky)/cholesky | solution.py:10
  313.3 4.9 %custom-call.6 = f32[1,64,64]{1,2,0:T(8,128)S(1)} custom-call(f32[1,64,64]{2,1,0:T(8,128)S(1)} %fusion.17), custom_call_target="InvertDiagBlocksLowerTriangular" | custom-call | tf_op jit(solution)/shard_map/jit(_solve_triangular)/triangular_solve | solution.py:11
  320.9 6.6 %fusion.27 = f32[512,64]{0,1:T(8,128)} fusion(f32[2560,512]{1,0:T(8,128)} %copy-done.1, f32[64,2560]{1,0:T(8,128)S(1)} %fusion.14), kind=kOutput, calls=%fused_computation.53 | convolution fusion | flops 1006632960 | bytes 6029312 | tf_op jit(solution)/shard_map/dot_general | solution.py:88
  327.5 8.5 %fusion.30 = f32[512,64]{0,1:T(8,128)} fusion(f32[512,2560]{1,0:T(8,128)} %copy-done.2, f32[64,2560]{1,0:T(8,128)S(1)} %fusion.12), kind=kOutput, calls=%fused_computation.56 | convolution fusion | flops 1006632960 | bytes 6029312 | tf_op jit(solution)/shard_map/dot_general | solution.py:89
  336.0 52.8 %all-reduce.7.cloned.1.call-done = (f32[512,64]{0,1:T(8,128)}, f32[512,64]{0,1:T(8,128)}) async-done(((f32[512,64]{0,1:T(8,128)}, f32[512,64]{0,1:T(8,128)}), (f32[512,64]{0,1:T(8,128)}, f32[512,64]{0,1:T(8,128)})) %all-reduce.7.cloned.1.call-update) | async-done | bytes 262160 | tf_op jit(solution)/shard_map/psum | solution.py:90
  389.9 8.0 %fusion.3 = (bf16[1,2560,512]{2,1,0:T(8,128)(2,1)}, bf16[2560,512]{1,0:T(8,128)(2,1)}) fusion(f32[2560,512]{1,0:T(8,128)} %copy-done.1, f32[64,2560]{1,0:T(8,128)} %copy-done.6, f32[512,64]{0,1:T(8,128)S(1)} %get-tuple-element.19), kind=kOutput, calls=%fused_computation.10 | convolution fusion | flops 1010565120 | bytes 11272192 | tf_op jit(solution)/shard_map/dot_general | solution.py:94
  397.9 7.8 %fusion.4 = (bf16[1,512,2560]{2,1,0:T(8,128)(2,1)}, bf16[512,2560]{1,0:T(8,128)(2,1)}) fusion(f32[512,2560]{1,0:T(8,128)} %copy-done.2, f32[512,64]{0,1:T(8,128)S(1)} %get-tuple-element.18, f32[64,2560]{1,0:T(8,128)S(1)} %fusion.12), kind=kOutput, calls=%fused_computation.11 | convolution fusion | flops 1010565120 | bytes 11272192 | tf_op jit(solution)/shard_map/dot_general | solution.py:95
  (58 shorter events, 19.2 us)
Async XLA Ops:
  7.2 72.4 %copy-start = (bf16[2560,512]{1,0:T(8,128)(2,1)S(1)}, bf16[2560,512]{1,0:T(8,128)(2,1)}, u32[]{:S(2)}) copy-start(bf16[2560,512]{1,0:T(8,128)(2,1)} %param.21) | copy-start | bytes 7864324
  7.2 72.4 %all-gather.3.cloned.1.call-start = ((), (), s32[]{:S(2)}) async-start(), calls=%async_computation | async-start | bytes 3276800 | tf_op jit(solution)/shard_map/all_gather | solution.py:45
  26.6 108.0 %all-gather.5.cloned.1.call-start = ((), (), s32[]{:S(2)}) async-start(), calls=%async_computation.1 | async-start | bytes 3276800 | tf_op jit(solution)/shard_map/all_gather | solution.py:46
  27.3 260.8 %all-reduce.5.cloned.1.call-start = ((), (), s32[]{:S(2)}) async-start(), calls=%async_computation.2 | async-start | bytes 2621440 | tf_op jit(solution)/shard_map/psum | solution.py:85
  27.4 4.1 copy-start.5
  79.6 3.5 copy-start.3
  134.6 4.3 %copy-start.4 = (bf16[8,512,512]{2,1,0:T(8,128)(2,1)S(1)}, bf16[8,512,512]{2,1,0:T(8,128)(2,1)}, u32[]{:S(2)}) copy-start(bf16[8,512,512]{2,1,0:T(8,128)(2,1)} %fusion.2) | copy-start | bytes 12582916
  138.9 1.7 copy-start.9
  138.9 2.5 copy-start.10
  141.4 1.7 copy-start.13
  143.1 4.4 %copy-start.2 = (f32[512,2560]{1,0:T(8,128)}, f32[512,2560]{1,0:T(8,128)S(1)}, u32[]{:S(2)}) copy-start(f32[512,2560]{1,0:T(8,128)S(1)} %convert_add_fusion) | copy-start | bytes 15728644
  143.1 4.4 %copy-start.7 = (bf16[1,2560,512]{2,1,0:T(8,128)(2,1)S(1)}, bf16[1,2560,512]{2,1,0:T(8,128)(2,1)}, u32[]{:S(2)}) copy-start(bf16[1,2560,512]{2,1,0:T(8,128)(2,1)} %param.23) | copy-start | bytes 7864324
  143.1 4.4 %copy-start.8 = (bf16[512,2560]{1,0:T(8,128)(2,1)S(1)}, bf16[512,2560]{1,0:T(8,128)(2,1)}, u32[]{:S(2)}) copy-start(bf16[512,2560]{1,0:T(8,128)(2,1)} %all-gather.3.cloned.1.call-done) | copy-start | bytes 7864324
  147.5 3.9 copy-start.14
  149.1 2.3 copy-start.1
  157.7 231.1 %all-reduce.7.cloned.1.call-start = ((), (), s32[]{:S(2)}) async-start(), calls=%async_computation.3 | async-start | bytes 524288 | tf_op jit(solution)/shard_map/psum | solution.py:90
  320.1 0.8 copy-start.6
  389.9 8.0 %copy-start.12 = (f32[512,64]{0,1:T(8,128)}, f32[512,64]{0,1:T(8,128)S(1)}, u32[]{:S(2)}) copy-start(f32[512,64]{0,1:T(8,128)S(1)} %get-tuple-element.19) | copy-start | bytes 393220
  389.9 8.0 %copy-start.11 = (f32[512,64]{0,1:T(8,128)}, f32[512,64]{0,1:T(8,128)S(1)}, u32[]{:S(2)}) copy-start(f32[512,64]{0,1:T(8,128)S(1)} %get-tuple-element.18) | copy-start | bytes 393220
Sparse Core Ops, SparseCore 0:
  26.7 52.8 all-gather.2
  81.2 53.3 all-gather.4
  157.9 130.1 all-reduce.4
  336.2 52.6 all-reduce.6
where the time goes:
time: 413 us; the launch traced here: 412 us
  waiting for transfers between devices  276 us (67%)
  matrix products  65 us (16%)
  other arithmetic  37.3 us (9%)
  between operations  14.8 us (4%)
  blocking collectives  13.4 us (3%)
  local copies, waits for them, and re-layouts  5.09 us (1%)
    psum x1, waiting for transfers between devices, shards(): sum_value, sum_out = lax.psum((p_value, p_out), ('rep', 'mdl'))  130 us
    psum x1, waiting for transfers between devices, shards(): total_value, total_out = lax.psum((term_value, term_out), 'rep')  52.8 us
    all_gather x1, waiting for transfers between devices, shards(): dy_whole = lax.all_gather(cotangent, 'mdl', axis=2, tiled=True)  50.1 us
    all_gather x1, waiting for transfers between devices, shards(): normed = lax.all_gather(normed_local, 'mdl', axis=1, tiled=True)  42.5 us
    psum x1, blocking collectives, shards(): totals = lax.psum(squares, 'mdl')  13.4 us
    another operation x6, other arithmetic, orthonormal_rows(): lower = jnp.linalg.cholesky(gram)  13 us
    another operation x4, other arithmetic, orthonormal_rows(): return jax.scipy.linalg.solve_triangular(lower, rows_part.T, lower=True).T  11.1 us
    dot_general x1, matrix products, shards(): term_out = jnp.dot(mem_out, phat_out, precision=HIGH)  8.54 us
  transfers between devices with their start and end apart: 4, of which 4 were waited for; matrix products, arithmetic and copies ran while one was open for 3% of the time, Pallas kernels for 0%

commit v1 on v0

v1 whole, which is shorter than its diff:
```python
import functools

import jax
import jax.numpy as jnp
from jax import lax
from jax.experimental import pallas as pl
from jax.experimental.pallas import tpu as pltpu
from jax.sharding import PartitionSpec as P

HIGH = lax.Precision.HIGH
HIGHEST = lax.Precision.HIGHEST
MESH = pl.DeviceIdType.MESH
VMEM_LIMIT = 48 * 1024 * 1024


def position(chips, depth):
    me = lax.axis_index("rep")
    core = lax.rem(me, 2)
    chip = me // 2
    z = lax.axis_index("mdl")
    return me, core, chip, z


def remote(src, dst, send, recv, rep, z):
    return pltpu.make_async_remote_copy(
        src_ref=src,
        dst_ref=dst,
        send_sem=send,
        recv_sem=recv,
        device_id=(rep, z),
        device_id_type=MESH,
    )


def greet(chips, depth):
    me, core, chip, z = position(chips, depth)
    barrier = pltpu.get_barrier_semaphore()
    peers = [(chip * 2 + 1 - core, z)]
    for k in range(1, chips):
        peers.append((lax.rem(chip + k, chips) * 2 + core, z))
    for j in range(1, depth):
        peers.append((me, lax.rem(z + j, depth)))
    for peer in peers:
        pl.semaphore_signal(barrier, inc=1, device_id=peer, device_id_type=MESH)
    pl.semaphore_wait(barrier, len(peers))


def table_kernel(chips, depth, rows_ref, gain_ref, out_ref, gout_ref, sz, rz, sg, rg, sp, rp, sc, rc, local):
    me, core, chip, z = position(chips, depth)
    sibling = chip * 2 + 1 - core
    own = pltpu.make_async_copy(rows_ref, out_ref.at[z], local.at[0])
    own.start()
    own_gain = pltpu.make_async_copy(gain_ref, gout_ref.at[z], local.at[1])
    own_gain.start()
    greet(chips, depth)
    sends = []
    along = {}
    for j in range(1, depth):
        to = lax.rem(z + j, depth)
        copy = remote(rows_ref.at[me], out_ref.at[z, me], sz.at[j], rz.at[j], me, to)
        copy.start()
        gain = remote(gain_ref, gout_ref.at[z], sg.at[j], rg.at[j], me, to)
        gain.start()
        along[j] = (copy, gain)
        sends += [copy, gain]
    waits = []
    plane = {}
    for j in range(1, depth):
        along[j][0].wait_recv()
        src = lax.rem(z - j + depth, depth)
        piece = out_ref.at[src, me]
        for k in range(1, chips):
            to = lax.rem(chip + k, chips) * 2 + core
            copy = remote(piece, piece, sp.at[k, j], rp.at[k, j], to, z)
            copy.start()
            plane[k, j] = copy
            sends.append(copy)
        copy = remote(piece, piece, sc.at[0, j], rc.at[0, j], sibling, z)
        copy.start()
        waits.append(copy)
        sends.append(copy)
    for j in range(1, depth):
        src = lax.rem(z - j + depth, depth)
        for k in range(1, chips):
            plane[k, j].wait_recv()
            owner = lax.rem(chip - k + chips, chips) * 2 + core
            piece = out_ref.at[src, owner]
            copy = remote(piece, piece, sc.at[k, j], rc.at[k, j], sibling, z)
            copy.start()
            waits.append(copy)
            sends.append(copy)
    own.wait()
    own_gain.wait()
    for j in range(1, depth):
        along[j][1].wait_recv()
    for copy in waits:
        copy.wait_recv()
    for copy in sends:
        copy.wait_send()


def gather_table(embedding, norm_gain, replicas, depth):
    chips = replicas // 2
    vocab, width = embedding.shape
    rows = embedding.reshape(replicas, vocab // replicas, width)
    gain = jnp.broadcast_to(norm_gain[None, :], (16, width))
    whole = jax.ShapeDtypeStruct((depth,) + rows.shape, rows.dtype)
    gains = jax.ShapeDtypeStruct((depth, 16, width), gain.dtype)
    sem = pltpu.SemaphoreType.DMA
    table, gains = pl.pallas_call(
        functools.partial(table_kernel, chips, depth),
        out_shape=(whole, gains),
        in_specs=[pl.BlockSpec(memory_space=pltpu.VMEM)] * 2,
        out_specs=[pl.BlockSpec(memory_space=pltpu.VMEM)] * 2,
        scratch_shapes=[
            sem((depth,)),
            sem((depth,)),
            sem((depth,)),
            sem((depth,)),
            sem((chips, depth)),
            sem((chips, depth)),
            sem((chips, depth)),
            sem((chips, depth)),
            sem((2,)),
        ],
        compiler_params=pltpu.CompilerParams(
            collective_id=0, has_side_effects=True, vmem_limit_bytes=VMEM_LIMIT
        ),
    )(rows, gain)
    table = table.reshape(depth, vocab, width).transpose(1, 0, 2).reshape(vocab, depth * width)
    return table, gains[:, 0, :].reshape(depth * width)


def reduce_steps(chips, depth, p_ref, out_ref, b1, b2, b3, sems, between):
    s1, r1, s2, r2, s3, r3, s4, r4, s5, r5, s6, r6 = sems
    me, core, chip, z = position(chips, depth)
    sibling = chip * 2 + 1 - core
    greet(chips, depth)
    sends = []
    first = remote(p_ref.at[1 - core], b1, s1.at[0], r1.at[0], sibling, z)
    first.start()
    sends.append(first)
    between(0)
    first.wait_recv()
    b1[...] = b1[...] + p_ref[core]
    group = []
    for k in range(1, chips):
        to = lax.rem(chip + k, chips)
        copy = remote(b1.at[to], b2.at[chip], s2.at[k], r2.at[k], to * 2 + core, z)
        copy.start()
        group.append(copy)
    sends += group
    between(1)
    total = b1[chip]
    for k in range(1, chips):
        group[k - 1].wait_recv()
        total = total + b2[lax.rem(chip - k + chips, chips)]
    if depth > 1:
        b2[chip] = total
        group = []
        for j in range(1, depth):
            to = lax.rem(z + j, depth)
            copy = remote(b2.at[chip, to], b3.at[z], s3.at[j], r3.at[j], me, to)
            copy.start()
            group.append(copy)
        sends += group
        total = b2[chip, z]
        for j in range(1, depth):
            group[j - 1].wait_recv()
            total = total + b3[lax.rem(z - j + depth, depth)]
        out_ref[core, chip, z] = total
    else:
        out_ref[core, chip] = total
    zz = z if depth > 1 else 0
    along = {}
    for j in range(1, depth):
        piece = out_ref.at[core, chip, zz]
        copy = remote(piece, piece, s4.at[j], r4.at[j], me, lax.rem(z + j, depth))
        copy.start()
        along[j] = copy
        sends.append(copy)
    waits = []
    plane = {}
    for j in range(depth):
        if j:
            along[j].wait_recv()
        src = lax.rem(zz - j + depth, depth) if depth > 1 else 0
        piece = out_ref.at[core, chip, src]
        for k in range(1, chips):
            to = lax.rem(chip + k, chips) * 2 + core
            copy = remote(piece, piece, s5.at[k, j], r5.at[k, j], to, z)
            copy.start()
            plane[k, j] = copy
            sends.append(copy)
        copy = remote(piece, piece, s6.at[0, j], r6.at[0, j], sibling, z)
        copy.start()
        waits.append(copy)
        sends.append(copy)
    between(2)
    for j in range(depth):
        src = lax.rem(zz - j + depth, depth) if depth > 1 else 0
        for k in range(1, chips):
            plane[k, j].wait_recv()
            piece = out_ref.at[core, lax.rem(chip - k + chips, chips), src]
            copy = remote(piece, piece, s6.at[k, j], r6.at[k, j], sibling, z)
            copy.start()
            waits.append(copy)
            sends.append(copy)
    between(3)
    for copy in waits:
        copy.wait_recv()
    for copy in sends:
        copy.wait_send()


def reduce_scratch(chips, depth, rows):
    sem = pltpu.SemaphoreType.DMA
    return [
        pltpu.VMEM((chips, depth, rows, 128), jnp.float32),
        pltpu.VMEM((chips, depth, rows, 128), jnp.float32),
        pltpu.VMEM((depth, rows, 128), jnp.float32),
        sem((1,)),
        sem((1,)),
        sem((chips,)),
        sem((chips,)),
        sem((depth,)),
        sem((depth,)),
        sem((depth,)),
        sem((depth,)),
        sem((chips, depth)),
        sem((chips, depth)),
        sem((chips, depth)),
        sem((chips, depth)),
    ]


def left_kernel(chips, depth, p_ref, out_ref, b1, b2, b3, *sems):
    reduce_steps(chips, depth, p_ref, out_ref, b1, b2, b3, sems, lambda stage: None)


def reduce_left(p, replicas, depth):
    chips = replicas // 2
    rows = p.shape[0] // (2 * chips * depth)
    shape = (2, chips, depth, rows, 128)
    out = pl.pallas_call(
        functools.partial(left_kernel, chips, depth),
        out_shape=jax.ShapeDtypeStruct(shape, jnp.float32),
        in_specs=[pl.BlockSpec(memory_space=pltpu.VMEM)],
        out_specs=pl.BlockSpec(memory_space=pltpu.VMEM),
        scratch_shapes=reduce_scratch(chips, depth, rows),
        compiler_params=pltpu.CompilerParams(
            collective_id=1, has_side_effects=True, vmem_limit_bytes=VMEM_LIMIT
        ),
    )(p.reshape(shape))
    return out.reshape(p.shape)


def factor_steps(work, rank, begin, end):
    tiles = [[work[h * rank + 8 * t : h * rank + 8 * t + 8, :] for t in range(rank // 8)] for h in range(2)]
    lines = lax.broadcasted_iota(jnp.int32, (8, 128), 0)
    for j in range(begin, end):
        at, line = divmod(j, 8)
        for h in range(2):
            lane = j + (rank if h == 0 else 0)
            part = tiles[h]
            pivot = part[at][line : line + 1, lane : lane + 1]
            inverse = 1.0 / jnp.sqrt(pivot)
            row = part[at][line : line + 1, :] * inverse
            for t in range(at, rank // 8):
                tile = part[t]
                column = tile[:, lane : lane + 1] * inverse
                fresh = tile - column * row
                if t == at:
                    fresh = jnp.where(lines > line, fresh, jnp.where(lines == line, row, tile))
                part[t] = fresh
    for h in range(2):
        for t in range(rank // 8):
            work[h * rank + 8 * t : h * rank + 8 * t + 8, :] = tiles[h][t]


def right_kernel(chips, rank, p_ref, gram_ref, out_ref, low_ref, b1, b2, b3, work, *sems):
    def between(stage):
        if stage == 0:
            work[...] = gram_ref[...]
        factor_steps(work, rank, stage * rank // 4, (stage + 1) * rank // 4)

    reduce_steps(chips, 1, p_ref, out_ref, b1, b2, b3, sems, between)
    lanes = lax.broadcasted_iota(jnp.int32, (rank, 128), 1)
    low_ref[:rank, :] = jnp.where(lanes < rank, work[:rank, :], 0.0)
    low_ref[rank:, :] = jnp.where(lanes >= rank, work[rank:, :], 0.0)


def reduce_right(p, gram, replicas):
    chips = replicas // 2
    rank = gram.shape[0] // 2
    rows = p.shape[0] // (2 * chips)
    shape = (2, chips, 1, rows, 128)
    eye = jnp.eye(rank, dtype=jnp.float32)
    start = jnp.concatenate(
        [
            jnp.concatenate([eye, gram[:rank, :rank]], axis=1),
            jnp.concatenate([gram[rank:, rank:], eye], axis=1),
        ],
        axis=0,
    )
    out, low = pl.pallas_call(
        functools.partial(right_kernel, chips, rank),
        out_shape=(
            jax.ShapeDtypeStruct(shape, jnp.float32),
            jax.ShapeDtypeStruct((2 * rank, 128), jnp.float32),
        ),
        in_specs=[pl.BlockSpec(memory_space=pltpu.VMEM)] * 2,
        out_specs=[pl.BlockSpec(memory_space=pltpu.VMEM)] * 2,
        scratch_shapes=(lambda s: s[:3] + [pltpu.VMEM((2 * rank, 128), jnp.float32)] + s[3:])(
            reduce_scratch(chips, 1, rows)
        ),
        compiler_params=pltpu.CompilerParams(
            collective_id=2, has_side_effects=True, vmem_limit_bytes=VMEM_LIMIT
        ),
    )(p.reshape(shape), start)
    return out.reshape(p.shape), low


def shards(
    replicas,
    depth,
    token_ids,
    lengths,
    embedding,
    norm_gain,
    scores,
    cotangent,
    w_value,
    w_out,
    err_value,
    err_out,
    q_value,
    q_out,
):
    samples, seq = token_ids.shape
    vocab = embedding.shape[0]
    rows = samples * seq
    rank = q_value.shape[1]
    dy_whole = lax.all_gather(cotangent, "mdl", axis=2, tiled=True)
    width_full = dy_whole.shape[2]
    raw, gain = gather_table(embedding, norm_gain, replicas, depth)
    raw = raw.astype(jnp.float32)
    scale = lax.rsqrt(jnp.sum(raw * raw, axis=1) / width_full + 1e-06)
    table = (raw * scale[:, None] * gain.astype(jnp.float32)[None, :]).astype(jnp.bfloat16)
    flat_ids = token_ids.reshape(rows)
    onehot = (flat_ids[:, None] == jnp.arange(vocab, dtype=jnp.int32)[None, :]).astype(jnp.bfloat16)
    normed = jnp.dot(onehot, table, preferred_element_type=jnp.float32).astype(jnp.bfloat16)
    live = jnp.arange(seq, dtype=jnp.int32)[None, :] < lengths[:, None]
    heads_local = scores.shape[1]
    inner_local = w_value.shape[1]
    head_size = inner_local // heads_local
    values = jnp.dot(normed, w_value, preferred_element_type=jnp.float32).astype(jnp.bfloat16)
    logits = jnp.where(live[:, None, None, :], scores.astype(jnp.float32), jnp.float32(-1e30))
    top = jnp.max(logits, axis=-1, keepdims=True)
    expo = jnp.exp(logits - top)
    weights = (expo / jnp.sum(expo, axis=-1, keepdims=True)).astype(jnp.bfloat16)
    values4 = values.reshape(samples, seq, heads_local, head_size)
    context = (
        jnp.einsum("shqk,skhd->sqhd", weights, values4, preferred_element_type=jnp.float32)
        .astype(jnp.bfloat16)
        .reshape(rows, inner_local)
    )
    dy_rows = jnp.where(live[..., None], dy_whole, jnp.zeros_like(dy_whole)).reshape(
        rows, width_full
    )
    dcontext = lax.dot_general(
        dy_rows, w_out, (((1,), (1,)), ((), ())), preferred_element_type=jnp.float32
    ).astype(jnp.bfloat16)
    dctx4 = dcontext.reshape(samples, seq, heads_local, head_size)
    dvalues = (
        jnp.einsum("shqk,sqhd->skhd", weights, dctx4, preferred_element_type=jnp.float32)
        .astype(jnp.bfloat16)
        .reshape(rows, inner_local)
    )
    grad_out = lax.dot_general(
        context, dy_rows, (((0,), (0,)), ((), ())), preferred_element_type=jnp.float32
    )
    grad_value = lax.dot_general(
        normed, dvalues, (((0,), (0,)), ((), ())), preferred_element_type=jnp.float32
    )
    mem_value = grad_value + err_value[0].astype(jnp.float32)
    mem_out = grad_out + err_out[0].astype(jnp.float32)
    p_value = jnp.dot(mem_value, q_value, precision=HIGH)
    p_out = lax.dot_general(mem_out, q_out, (((0,), (0,)), ((), ())), precision=HIGH)
    p_both = reduce_left(jnp.concatenate([p_value, p_out], axis=1), replicas, depth)
    gram = lax.dot_general(p_both, p_both, (((0,), (0,)), ((), ())), precision=HIGHEST)
    term_value = lax.dot_general(
        mem_value, p_both[:, :rank], (((0,), (0,)), ((), ())), precision=HIGH
    )
    term_out = jnp.dot(mem_out, p_both[:, rank:], precision=HIGH)
    terms, low = reduce_right(jnp.concatenate([term_value, term_out], axis=1), gram, replicas)
    phat = lax.dot_general(p_both, low, (((1,), (1,)), ((), ())), precision=HIGHEST)
    new_q = lax.dot_general(terms, low, (((1,), (1,)), ((), ())), precision=HIGHEST) / replicas
    new_q_value = new_q[:, :rank]
    new_q_out = new_q[:, rank:]
    full_value = lax.dot_general(
        phat[:, :rank], new_q_value, (((1,), (1,)), ((), ())), precision=HIGH
    )
    full_out = lax.dot_general(
        new_q_out, phat[:, rank:], (((1,), (1,)), ((), ())), precision=HIGH
    )
    new_err_value = (mem_value - full_value).astype(jnp.bfloat16)[None]
    new_err_out = (mem_out - full_out).astype(jnp.bfloat16)[None]
    return (
        full_value.astype(jnp.bfloat16),
        full_out.astype(jnp.bfloat16),
        new_err_value,
        new_err_out,
        new_q_value,
        new_q_out,
    )


def solution(mesh):
    return jax.shard_map(
        functools.partial(shards, mesh.shape["rep"], mesh.shape["mdl"]),
        mesh=mesh,
        in_specs=(
            P("rep", None),
            P("rep"),
            P(None, "mdl"),
            P("mdl"),
            P("rep", "mdl", None, None),
            P("rep", None, "mdl"),
            P(None, "mdl"),
            P("mdl", None),
            P("rep", None, "mdl"),
            P("rep", "mdl", None),
            P("mdl", None),
            P("mdl", None),
        ),
        out_specs=(
            P(None, "mdl"),
            P("mdl", None),
            P("rep", None, "mdl"),
            P("rep", "mdl", None),
            P("mdl", None),
            P("mdl", None),
        ),
        check_vma=False,
    )
```

time: 413 us -> 165 us (0.40)
  waiting for transfers between devices: 276 us -> 14.4 us
  Pallas kernels: 0 us -> 66.4 us
  matrix products: 65 us -> 38.8 us
  other arithmetic: 37.3 us -> 11.2 us
  local copies, waits for them, and re-layouts: 5.09 us -> 18.8 us
  blocking collectives: 13.4 us -> 0 us
    psum x2 -> x0, waiting for transfers between devices: 183 us -> none  [the longest x1 130 us: shards(): sum_value, sum_out = lax.psum((p_value, p_out), ('rep', 'mdl'))]
    pallas_call x0 -> x3, Pallas kernels: none -> 66.4 us  [the longest x1 30.3 us: reduce_left(): pl.pallas_call(functools.partial(left_kernel, chips, depth), out_shape=ja...]
    all_gather x1 -> x0, waiting for transfers between devices: 42.5 us -> none  [shards(): normed = lax.all_gather(normed_local, 'mdl', axis=1, tiled=True)]
    all_gather x1, waiting for transfers between devices: 50.1 us -> 13.7 us  [shards(): dy_whole = lax.all_gather(cotangent, 'mdl', axis=2, tiled=True)]
    another operation x11 -> x1, other arithmetic: 27.8 us -> 2.29 us  [the longest x6 13 us: orthonormal_rows(): lower = jnp.linalg.cholesky(gram)]
    dot_general x7 -> x8, matrix products: 37.5 us -> 23.3 us  [the longest x1 7.4 us: shards(): lax.dot_general(new_q_out, phat[:, rank:], (((1,), (1,)), ((), ())), prec...]
    psum x1 -> x0, blocking collectives: 13.4 us -> none  [shards(): totals = lax.psum(squares, 'mdl')]
    unnamed x30 -> x48, local copies, waits for them, and re-layouts: 4.94 us -> 10.7 us
  transfers between devices with their start and end apart: 4 -> 1, of which waited for: 4 -> 1; matrix products, arithmetic and copies ran while one was open for 3% -> 12% of each run, Pallas kernels for 0% -> 13%
where the time goes in v1:
time: 165 us
  Pallas kernels  66.4 us (40%)
  matrix products  38.8 us (24%)
  local copies, waits for them, and re-layouts  18.8 us (11%)
  between operations  15.1 us (9%)
  waiting for transfers between devices  14.4 us (9%)
  other arithmetic  11.2 us (7%)
    pallas_call x1, Pallas kernels, reduce_left(): pl.pallas_call(functools.partial(left_kernel, chips, depth), out_shape=ja...  30.3 us
    pallas_call x1, Pallas kernels, gather_table(): pl.pallas_call(functools.partial(table_kernel, chips, depth), out_shape=(...  20.6 us
    pallas_call x1, Pallas kernels, reduce_right(): pl.pallas_call(functools.partial(right_kernel, chips, rank), out_shape=(j...  15.4 us
    all_gather x1, waiting for transfers between devices, shards(): dy_whole = lax.all_gather(cotangent, 'mdl', axis=2, tiled=True)  13.7 us
    unnamed x48, local copies, waits for them, and re-layouts  10.7 us
    dot_general x1, matrix products, shards(): lax.dot_general(new_q_out, phat[:, rank:], (((1,), (1,)), ((), ())), prec...  7.4 us
    dot_general x1, matrix products, shards(): lax.dot_general(phat[:, :rank], new_q_value, (((1,), (1,)), ((), ())), pr...  4.73 us
    convert_element_type x1, local copies, waits for them, and re-layouts, shards(): raw = raw.astype(jnp.float32)  4.31 us
  transfers between devices with their start and end apart: 1, of which 1 were waited for; matrix products, arithmetic and copies ran while one was open for 12% of the time, Pallas kernels for 13%

profile of v1, /device:TPU:0, one launch (start us, length us, event | category | flops | bytes accessed | tf_op | source)
XLA Modules:
  0.0 164.6 jit_solution(11994327186476724130)
XLA Ops:
  10.3 20.6 %shard_map.163 = (bf16[4,8,48,640]{3,2,1,0:T(8,128)(2,1)S(1)}, bf16[4,16,640]{2,1,0:T(8,128)(2,1)S(1)}) custom-call(bf16[8,48,640]{2,1,0:T(8,128)(2,1)S(1)} %bitcast.84, bf16[16,640]{1,0:T(8,128)(2,1)S(1)} %broadcast_in_dim.28.gain_ref), custom_call_target="tpu_custom_call" | custom-call | tf_op jit(solution)/shard_map/pallas_call | solution.py:110
  32.3 2.0 %multiply_reduce_fusion = f32[8,48]{1,0:T(8,128)S(1)} fusion(bf16[4,8,48,640]{3,2,1,0:T(8,128)(2,1)} %copy-done.2), kind=kLoop, calls=%fused_computation.14 | loop fusion | flops 2948736 | bytes 1967616 | tf_op jit(solution)/shard_map/reduce_sum | solution.py:348
  34.4 4.3 %copy.20 = f32[4,384,640]{1,2,0:T(8,128)} copy(bf16[4,384,640]{2,1,0:T(8,128)(2,1)} %bitcast.81) | data formatting | bytes 5898240 | tf_op jit(solution)/shard_map/convert_element_type | solution.py:347
  38.7 2.6 %fusion.4 = bf16[384,2560]{0,1:T(8,128)(2,1)S(1)} fusion(f32[4,384,640]{1,2,0:T(8,128)} %copy.20, f32[2560]{0:T(1024)S(1)} %reshape.122, f32[384]{0:T(512)S(1)} %reshape.127), kind=kLoop, calls=%fused_computation.13 | loop fusion | flops 2949120 | bytes 5910016 | tf_op jit(solution)/shard_map/convert_element_type | solution.py:349
  41.4 1.6 convolution_convert_fusion
  44.4 1.6 convolution_convert_fusion.3
  46.0 2.1 %fusion.1 = f32[8,512]{1,0:T(8,128)S(1)} fusion(bf16[1,8,512,512]{3,2,1,0:T(8,128)(2,1)S(1)} %copy-done.11, f32[8,512]{1,0:T(8,128)S(1)} %fusion, pred[512]{0:T(512)(128)(4,1)S(1)} %iota_compare_fusion.3), kind=kLoop, calls=%fused_computation.4 | loop fusion | flops 8384512 | bytes 4227584 | tf_op jit(solution)/shard_map/reduce_sum | solution.py:361
  48.1 2.3 %fusion.2 = bf16[8,512,512]{2,1,0:T(8,128)(2,1)S(1)} fusion(bf16[1,8,512,512]{3,2,1,0:T(8,128)(2,1)S(1)} %copy-done.11, f32[8,512]{1,0:T(8,128)S(1)} %fusion.1, f32[8,512]{1,0:T(8,128)S(1)} %fusion, pred[512]{0:T(512)(128)(4,1)S(1)} %iota_compare_fusion.3), kind=kLoop, calls=%fused_computation.10 | loop fusion | flops 10485760 | bytes 8421888 | tf_op jit(solution)/shard_map/reshape.6
  50.4 1.9 %copy-done.9 = bf16[8,512,512]{2,1,0:T(8,128)(2,1)} copy-done((bf16[8,512,512]{2,1,0:T(8,128)(2,1)}, bf16[8,512,512]{2,1,0:T(8,128)(2,1)S(1)}, u32[]{:S(2)}) %copy-start.9) | copy-done | bytes 4194328
  53.7 13.7 %all-gather.2.cloned.1.call-done = bf16[1,512,2560]{2,1,0:T(8,128)(2,1)} async-done(((bf16[1,512,640]{2,1,0:T(8,128)(2,1)}), bf16[1,512,2560]{2,1,0:T(8,128)(2,1)}) %all-gather.2.cloned.1.call-update) | async-done | bytes 2621456 | tf_op jit(solution)/shard_map/all_gather | solution.py:344
  67.4 4.3 %fusion.14 = bf16[512,512]{0,1:T(8,128)(2,1)S(1)} fusion(bf16[512,2560]{1,0:T(8,128)(2,1)} %param.19, bf16[1,512,2560]{2,1,0:T(8,128)(2,1)} %all-gather.2.cloned.1.call-done, pred[512]{0:T(512)(128)(4,1)S(1)} %iota_compare_fusion.3), kind=kOutput, calls=%fused_computation.28 | convolution fusion | flops 1343750144 | bytes 5767680 | tf_op jit(solution)/shard_map/dot_general | solution.py:371
  74.3 1.6 %convert_add_fusion = f32[512,2560]{1,0:T(8,128)S(1)} fusion(bf16[512,512]{0,1:T(8,128)(2,1)S(1)} %bitcast.88, bf16[1,512,2560]{2,1,0:T(8,128)(2,1)S(1)} %copy-done.15, bf16[1,512,2560]{2,1,0:T(8,128)(2,1)S(1)} %copy-done.16, pred[512]{0:T(512)(128)(4,1)S(1)} %iota_compare_fusion.3), kind=kOutput, calls=%fused_computation.5 | convolution fusion | flops 1346109440 | bytes 11010560 | tf_op jit(solution)/shard_map/dot_general | solution.py:380
  76.0 1.6 %fusion.32 = f32[2560,64]{0,1:T(8,128)S(1)} fusion(f32[512,2560]{1,0:T(8,128)S(1)} %convert_add_fusion, f32[512,64]{0,1:T(8,128)S(1)} %copy-done.19), kind=kOutput, calls=%fused_computation.50 | convolution fusion | flops 503316480 | bytes 6029312 | tf_op jit(solution)/shard_map/dot_general | solution.py:389
  80.4 1.6 convert_add_fusion.1
  82.0 2.5 %fusion.31 = f32[2560,64]{0,1:T(8,128)S(1)} fusion(f32[2560,512]{1,0:T(8,128)S(1)} %convert_add_fusion.1, f32[512,64]{0,1:T(8,128)S(1)} %copy-done.20), kind=kOutput, calls=%fused_computation.49 | convolution fusion | flops 503316480 | bytes 6029312 | tf_op jit(solution)/shard_map/dot_general | solution.py:388
  85.7 2.8 %copy.21 = f32[2560,128]{1,0:T(8,128)} copy(f32[2560,128]{0,1:T(8,128)} %pad_maximum_fusion) | data formatting | bytes 2621440 | tf_op jit(solution)/shard_map/concatenate | solution.py:390
  89.8 30.3 %shard_map.164 = f32[2,4,4,80,128]{4,3,2,1,0:T(8,128)S(1)} custom-call(f32[2,4,4,80,128]{4,3,2,1,0:T(8,128)S(1)} %bitcast.82), custom_call_target="tpu_custom_call" | custom-call | tf_op jit(solution)/shard_map/pallas_call | solution.py:245
  120.1 2.2 %convolution_bitcast_fusion = f32[128,128]{1,0:T(8,128)S(1)} fusion(f32[2,4,4,80,128]{4,3,2,1,0:T(8,128)S(1)} %shard_map.164), kind=kOutput, calls=%fused_computation.31 | convolution fusion | flops 503316480 | bytes 1376256 | tf_op jit(solution)/shard_map/dot_general | solution.py:391
  122.3 2.9 %fusion.10 = f32[512,64]{0,1:T(8,128)S(1)} fusion(f32[512,2560]{1,0:T(8,128)S(1)} %copy-done.8, f32[2560,128]{1,0:T(8,128)S(1)} %bitcast.78), kind=kOutput, calls=%fused_computation.21 | convolution fusion | flops 503316480 | bytes 6684672 | tf_op jit(solution)/shard_map/dot_general | solution.py:395
  125.2 1.5 fusion.12
  127.1 15.4 %shard_map.165 = (f32[2,4,1,64,128]{4,3,2,1,0:T(8,128)S(1)}, f32[128,128]{1,0:T(8,128)S(1)}) custom-call(f32[2,4,1,64,128]{4,3,2,1,0:T(8,128)S(1)} %bitcast.83, f32[128,128]{1,0:T(8,128)S(1)} %maximum_maximum_fusion.gram_ref), custom_call_target="tpu_custom_call" | custom-call | tf_op jit(solution)/shard_map/pallas_call | solution.py:306
  142.5 2.6 %fusion.33 = f32[2560,128]{0,1:T(8,128)S(1)} fusion(f32[2560,128]{1,0:T(8,128)} %bitcast.80, f32[128,128]{1,0:T(8,128)S(1)} %get-tuple-element.12), kind=kOutput, calls=%fused_computation.51 | convolution fusion | flops 503316480 | bytes 2686976 | tf_op jit(solution)/shard_map/dot_general | solution.py:397
  145.6 7.4 %fusion.6 = (bf16[1,512,2560]{2,1,0:T(8,128)(2,1)}, bf16[512,2560]{1,0:T(8,128)(2,1)}) fusion(f32[512,2560]{1,0:T(8,128)} %copy-done.7, f32[512,64]{0,1:T(8,128)S(1)} %get-tuple-element.18, f32[2560,128]{0,1:T(8,128)S(1)} %fusion.33), kind=kOutput, calls=%fused_computation.16 | convolution fusion | flops 507248640 | bytes 11272192 | tf_op jit(solution)/shard_map/dot_general | solution.py:404
  153.1 4.7 %fusion.5 = (bf16[1,2560,512]{2,1,0:T(8,128)(2,1)}, bf16[2560,512]{1,0:T(8,128)(2,1)}) fusion(f32[2560,512]{1,0:T(8,128)S(1)} %bitcast.87, f32[512,64]{0,1:T(8,128)S(1)} %get-tuple-element.19, f32[2560,128]{0,1:T(8,128)S(1)} %fusion.33), kind=kOutput, calls=%fused_computation.15 | convolution fusion | flops 507248640 | bytes 11272192 | tf_op jit(solution)/shard_map/dot_general | solution.py:401
  (67 shorter events, 15.2 us)
Async XLA Ops:
  7.2 37.3 %copy-start = (bf16[2560,512]{1,0:T(8,128)(2,1)S(1)}, bf16[2560,512]{1,0:T(8,128)(2,1)}, u32[]{:S(2)}) copy-start(bf16[2560,512]{1,0:T(8,128)(2,1)} %param.18) | copy-start | bytes 7864324
  7.2 60.3 %all-gather.2.cloned.1.call-start = ((), (), s32[]{:S(2)}) async-start(), calls=%async_computation | async-start | bytes 3276800 | tf_op jit(solution)/shard_map/all_gather | solution.py:344
  31.0 1.3 copy-start.2
  38.7 2.6 %copy-start.21 = (s32[1,512]{1,0:T(1,128)S(1)}, s32[1,512]{1,0:T(1,128)}, u32[]{:S(2)}) copy-start(s32[1,512]{1,0:T(1,128)} %param.12) | copy-start | bytes 6148
  41.3 2.2 %copy-start.11 = (bf16[1,8,512,512]{3,2,1,0:T(8,128)(2,1)S(1)}, bf16[1,8,512,512]{3,2,1,0:T(8,128)(2,1)}, u32[]{:S(2)}) copy-start(bf16[1,8,512,512]{3,2,1,0:T(8,128)(2,1)} %param.16) | copy-start | bytes 12582916
  43.5 2.5 %copy-start.13 = (bf16[512,2560]{1,0:T(8,128)(2,1)}, bf16[512,2560]{1,0:T(8,128)(2,1)S(1)}, u32[]{:S(2)}) copy-start(bf16[512,2560]{1,0:T(8,128)(2,1)S(1)} %convolution_convert_fusion) | copy-start | bytes 7864324
  50.4 1.9 %copy-start.9 = (bf16[8,512,512]{2,1,0:T(8,128)(2,1)}, bf16[8,512,512]{2,1,0:T(8,128)(2,1)S(1)}, u32[]{:S(2)}) copy-start(bf16[8,512,512]{2,1,0:T(8,128)(2,1)S(1)} %fusion.2) | copy-start | bytes 12582916
  67.4 4.3 %copy-start.10 = (bf16[8,512,512]{2,1,0:T(8,128)(2,1)S(1)}, bf16[8,512,512]{2,1,0:T(8,128)(2,1)}, u32[]{:S(2)}) copy-start(bf16[8,512,512]{2,1,0:T(8,128)(2,1)} %copy-done.9) | copy-start | bytes 12582916
  71.7 1.7 %copy-start.15 = (bf16[1,512,2560]{2,1,0:T(8,128)(2,1)S(1)}, bf16[1,512,2560]{2,1,0:T(8,128)(2,1)}, u32[]{:S(2)}) copy-start(bf16[1,512,2560]{2,1,0:T(8,128)(2,1)} %param.21) | copy-start | bytes 7864324
  71.8 2.5 %copy-start.16 = (bf16[1,512,2560]{2,1,0:T(8,128)(2,1)S(1)}, bf16[1,512,2560]{2,1,0:T(8,128)(2,1)}, u32[]{:S(2)}) copy-start(bf16[1,512,2560]{2,1,0:T(8,128)(2,1)} %all-gather.2.cloned.1.call-done) | copy-start | bytes 7864324
  74.3 1.7 %copy-start.19 = (f32[512,64]{0,1:T(8,128)S(1)}, f32[512,64]{0,1:T(8,128)}, u32[]{:S(2)}) copy-start(f32[512,64]{0,1:T(8,128)} %param.23) | copy-start | bytes 393220
  76.0 2.7 %copy-start.7 = (f32[512,2560]{1,0:T(8,128)}, f32[512,2560]{1,0:T(8,128)S(1)}, u32[]{:S(2)}) copy-start(f32[512,2560]{1,0:T(8,128)S(1)} %convert_add_fusion) | copy-start | bytes 15728644
  76.0 3.6 %copy-start.12 = (bf16[1,2560,512]{2,1,0:T(8,128)(2,1)S(1)}, bf16[1,2560,512]{2,1,0:T(8,128)(2,1)}, u32[]{:S(2)}) copy-start(bf16[1,2560,512]{2,1,0:T(8,128)(2,1)} %param.20) | copy-start | bytes 7864324
  76.0 4.4 %copy-start.14 = (bf16[512,2560]{1,0:T(8,128)(2,1)S(1)}, bf16[512,2560]{1,0:T(8,128)(2,1)}, u32[]{:S(2)}) copy-start(bf16[512,2560]{1,0:T(8,128)(2,1)} %copy-done.13) | copy-start | bytes 7864324
  80.4 1.6 copy-start.20
  82.0 2.5 %copy-start.5 = (f32[2560,512]{1,0:T(8,128)}, f32[2560,512]{1,0:T(8,128)S(1)}, u32[]{:S(2)}) copy-start(f32[2560,512]{1,0:T(8,128)S(1)} %convert_add_fusion.1) | copy-start | bytes 15728644
  88.4 1.3 copy-start.3
  89.8 32.5 %copy-start.8 = (f32[512,2560]{1,0:T(8,128)S(1)}, f32[512,2560]{1,0:T(8,128)}, u32[]{:S(2)}) copy-start(f32[512,2560]{1,0:T(8,128)} %copy-done.7) | copy-start | bytes 15728644
  120.0 5.2 %copy-start.1 = (f32[2,4,4,80,128]{4,3,2,1,0:T(8,128)}, f32[2,4,4,80,128]{4,3,2,1,0:T(8,128)S(1)}, u32[]{:S(2)}) copy-start(f32[2,4,4,80,128]{4,3,2,1,0:T(8,128)S(1)} %shard_map.164) | copy-start | bytes 3932164
  122.3 2.9 %copy-start.6 = (f32[2560,512]{1,0:T(8,128)S(1)}, f32[2560,512]{1,0:T(8,128)}, u32[]{:S(2)}) copy-start(f32[2560,512]{1,0:T(8,128)} %copy-done.5) | copy-start | bytes 15728644
  145.6 7.5 %slice-start = ((s8[5242880]{0:T(1024)(128)(4,1)}), s8[4194304]{0:T(1024)(128)(4,1)S(1)}, s32[]{:S(2)}) async-start(s8[5242880]{0:T(1024)(128)(4,1)} %bitcast.86), calls=%async_computation.1 | async-start | bytes 8388608
  145.6 7.4 %copy-start.17 = (f32[512,64]{0,1:T(8,128)}, f32[512,64]{0,1:T(8,128)S(1)}, u32[]{:S(2)}) copy-start(f32[512,64]{0,1:T(8,128)S(1)} %get-tuple-element.18) | copy-start | bytes 393220
  145.6 7.4 %copy-start.18 = (f32[512,64]{0,1:T(8,128)}, f32[512,64]{0,1:T(8,128)S(1)}, u32[]{:S(2)}) copy-start(f32[512,64]{0,1:T(8,128)S(1)} %get-tuple-element.19) | copy-start | bytes 393220
  145.6 7.4 %slice-start.1 = ((s8[5242880]{0:T(1024)(128)(4,1)}), s8[1048576]{0:T(1024)(128)(4,1)S(1)}, s32[]{:S(2)}) async-start(s8[5242880]{0:T(1024)(128)(4,1)} %bitcast.86), calls=%async_computation.2 | async-start | bytes 2097152
  (1 other events, 1.0 us)
Sparse Core Ops, SparseCore 0:
  9.6 57.7 all-gather.1

commit v2 on v1

--- a/solution.py
+++ b/solution.py
@@ -48,7 +48,14 @@
 def table_kernel(chips, depth, rows_ref, gain_ref, out_ref, gout_ref, sz, rz, sg, rg, sp, rp, sc, rc, local):
     me, core, chip, z = position(chips, depth)
     sibling = chip * 2 + 1 - core
-    own = pltpu.make_async_copy(rows_ref, out_ref.at[z], local.at[0])
+    width = rows_ref.shape[2]
+
+    def spot(owner, src):
+        return out_ref.at[owner, :, pl.ds(pl.multiple_of(src * width, 128), width)]
+
+    own = pltpu.make_async_copy(
+        rows_ref, out_ref.at[:, :, pl.ds(pl.multiple_of(z * width, 128), width)], local.at[0]
+    )
     own.start()
     own_gain = pltpu.make_async_copy(gain_ref, gout_ref.at[z], local.at[1])
     own_gain.start()
@@ -57,7 +64,7 @@
     along = {}
     for j in range(1, depth):
         to = lax.rem(z + j, depth)
-        copy = remote(rows_ref.at[me], out_ref.at[z, me], sz.at[j], rz.at[j], me, to)
+        copy = remote(rows_ref.at[me], spot(me, z), sz.at[j], rz.at[j], me, to)
         copy.start()
         gain = remote(gain_ref, gout_ref.at[z], sg.at[j], rg.at[j], me, to)
         gain.start()
@@ -68,7 +75,7 @@
     for j in range(1, depth):
         along[j][0].wait_recv()
         src = lax.rem(z - j + depth, depth)
-        piece = out_ref.at[src, me]
+        piece = spot(me, src)
         for k in range(1, chips):
             to = lax.rem(chip + k, chips) * 2 + core
             copy = remote(piece, piece, sp.at[k, j], rp.at[k, j], to, z)
@@ -84,7 +91,7 @@
         for k in range(1, chips):
             plane[k, j].wait_recv()
             owner = lax.rem(chip - k + chips, chips) * 2 + core
-            piece = out_ref.at[src, owner]
+            piece = spot(owner, src)
             copy = remote(piece, piece, sc.at[k, j], rc.at[k, j], sibling, z)
             copy.start()
             waits.append(copy)
@@ -104,7 +111,7 @@
     vocab, width = embedding.shape
     rows = embedding.reshape(replicas, vocab // replicas, width)
     gain = jnp.broadcast_to(norm_gain[None, :], (16, width))
-    whole = jax.ShapeDtypeStruct((depth,) + rows.shape, rows.dtype)
+    whole = jax.ShapeDtypeStruct(rows.shape[:2] + (depth * width,), rows.dtype)
     gains = jax.ShapeDtypeStruct((depth, 16, width), gain.dtype)
     sem = pltpu.SemaphoreType.DMA
     table, gains = pl.pallas_call(
@@ -127,7 +134,7 @@
             collective_id=0, has_side_effects=True, vmem_limit_bytes=VMEM_LIMIT
         ),
     )(rows, gain)
-    table = table.reshape(depth, vocab, width).transpose(1, 0, 2).reshape(vocab, depth * width)
+    table = table.reshape(vocab, depth * width)
     return table, gains[:, 0, :].reshape(depth * width)
 
 
@@ -142,7 +149,8 @@
     sends.append(first)
     between(0)
     first.wait_recv()
-    b1[...] = b1[...] + p_ref[core]
+    kind = p_ref.dtype
+    b1[...] = (b1[...].astype(jnp.float32) + p_ref[core].astype(jnp.float32)).astype(kind)
     group = []
     for k in range(1, chips):
         to = lax.rem(chip + k, chips)
@@ -151,12 +159,12 @@
         group.append(copy)
     sends += group
     between(1)
-    total = b1[chip]
+    total = b1[chip].astype(jnp.float32)
     for k in range(1, chips):
         group[k - 1].wait_recv()
-        total = total + b2[lax.rem(chip - k + chips, chips)]
+        total = total + b2[lax.rem(chip - k + chips, chips)].astype(jnp.float32)
     if depth > 1:
-        b2[chip] = total
+        b2[chip] = total.astype(kind)
         group = []
         for j in range(1, depth):
             to = lax.rem(z + j, depth)
@@ -164,13 +172,13 @@
             copy.start()
             group.append(copy)
         sends += group
-        total = b2[chip, z]
+        total = b2[chip, z].astype(jnp.float32)
         for j in range(1, depth):
             group[j - 1].wait_recv()
-            total = total + b3[lax.rem(z - j + depth, depth)]
-        out_ref[core, chip, z] = total
+            total = total + b3[lax.rem(z - j + depth, depth)].astype(jnp.float32)
+        out_ref[core, chip, z] = total.astype(kind)
     else:
-        out_ref[core, chip] = total
+        out_ref[core, chip] = total.astype(kind)
     zz = z if depth > 1 else 0
     along = {}
     for j in range(1, depth):
@@ -213,12 +221,12 @@
         copy.wait_send()
 
 
-def reduce_scratch(chips, depth, rows):
+def reduce_scratch(chips, depth, rows, kind):
     sem = pltpu.SemaphoreType.DMA
     return [
-        pltpu.VMEM((chips, depth, rows, 128), jnp.float32),
-        pltpu.VMEM((chips, depth, rows, 128), jnp.float32),
-        pltpu.VMEM((depth, rows, 128), jnp.float32),
+        pltpu.VMEM((chips, depth, rows, 128), kind),
+        pltpu.VMEM((chips, depth, rows, 128), kind),
+        pltpu.VMEM((depth, rows, 128), kind),
         sem((1,)),
         sem((1,)),
         sem((chips,)),
@@ -244,10 +252,10 @@
     shape = (2, chips, depth, rows, 128)
     out = pl.pallas_call(
         functools.partial(left_kernel, chips, depth),
-        out_shape=jax.ShapeDtypeStruct(shape, jnp.float32),
+        out_shape=jax.ShapeDtypeStruct(shape, p.dtype),
         in_specs=[pl.BlockSpec(memory_space=pltpu.VMEM)],
         out_specs=pl.BlockSpec(memory_space=pltpu.VMEM),
-        scratch_shapes=reduce_scratch(chips, depth, rows),
+        scratch_shapes=reduce_scratch(chips, depth, rows, p.dtype),
         compiler_params=pltpu.CompilerParams(
             collective_id=1, has_side_effects=True, vmem_limit_bytes=VMEM_LIMIT
         ),
@@ -312,7 +320,7 @@
         in_specs=[pl.BlockSpec(memory_space=pltpu.VMEM)] * 2,
         out_specs=[pl.BlockSpec(memory_space=pltpu.VMEM)] * 2,
         scratch_shapes=(lambda s: s[:3] + [pltpu.VMEM((2 * rank, 128), jnp.float32)] + s[3:])(
-            reduce_scratch(chips, 1, rows)
+            reduce_scratch(chips, 1, rows, p.dtype)
         ),
         compiler_params=pltpu.CompilerParams(
             collective_id=2, has_side_effects=True, vmem_limit_bytes=VMEM_LIMIT
@@ -341,8 +349,14 @@
     vocab = embedding.shape[0]
     rows = samples * seq
     rank = q_value.shape[1]
-    dy_whole = lax.all_gather(cotangent, "mdl", axis=2, tiled=True)
-    width_full = dy_whole.shape[2]
+    spot = lax.axis_index("mdl")
+    live = jnp.arange(seq, dtype=jnp.int32)[None, :] < lengths[:, None]
+    masked = jnp.where(live[..., None], cotangent, jnp.zeros_like(cotangent)).reshape(rows, -1)
+    width = masked.shape[1]
+    width_full = width * depth
+    pieces = [masked]
+    for j in range(1, depth):
+        pieces.append(lax.ppermute(masked, "mdl", [(i, (i + j) % depth) for i in range(depth)]))
     raw, gain = gather_table(embedding, norm_gain, replicas, depth)
     raw = raw.astype(jnp.float32)
     scale = lax.rsqrt(jnp.sum(raw * raw, axis=1) / width_full + 1e-06)
@@ -350,7 +364,6 @@
     flat_ids = token_ids.reshape(rows)
     onehot = (flat_ids[:, None] == jnp.arange(vocab, dtype=jnp.int32)[None, :]).astype(jnp.bfloat16)
     normed = jnp.dot(onehot, table, preferred_element_type=jnp.float32).astype(jnp.bfloat16)
-    live = jnp.arange(seq, dtype=jnp.int32)[None, :] < lengths[:, None]
     heads_local = scores.shape[1]
     inner_local = w_value.shape[1]
     head_size = inner_local // heads_local
@@ -365,9 +378,10 @@
         .astype(jnp.bfloat16)
         .reshape(rows, inner_local)
     )
-    dy_rows = jnp.where(live[..., None], dy_whole, jnp.zeros_like(dy_whole)).reshape(
-        rows, width_full
-    )
+    dy_rows = jnp.zeros((rows, width_full), jnp.bfloat16)
+    for j in (0, 1, 3, 2) if depth == 4 else range(depth):
+        source = lax.rem(spot - j + depth, depth)
+        dy_rows = lax.dynamic_update_slice(dy_rows, pieces[j], (0, source * width))
     dcontext = lax.dot_general(
         dy_rows, w_out, (((1,), (1,)), ((), ())), preferred_element_type=jnp.float32
     ).astype(jnp.bfloat16)
@@ -385,24 +399,50 @@
     )
     mem_value = grad_value + err_value[0].astype(jnp.float32)
     mem_out = grad_out + err_out[0].astype(jnp.float32)
-    p_value = jnp.dot(mem_value, q_value, precision=HIGH)
-    p_out = lax.dot_general(mem_out, q_out, (((0,), (0,)), ((), ())), precision=HIGH)
-    p_both = reduce_left(jnp.concatenate([p_value, p_out], axis=1), replicas, depth)
-    gram = lax.dot_general(p_both, p_both, (((0,), (0,)), ((), ())), precision=HIGHEST)
-    term_value = lax.dot_general(
-        mem_value, p_both[:, :rank], (((0,), (0,)), ((), ())), precision=HIGH
-    )
-    term_out = jnp.dot(mem_out, p_both[:, rank:], precision=HIGH)
-    terms, low = reduce_right(jnp.concatenate([term_value, term_out], axis=1), gram, replicas)
-    phat = lax.dot_general(p_both, low, (((1,), (1,)), ((), ())), precision=HIGHEST)
+    kept_value = mem_value.astype(jnp.bfloat16)
+    kept_out = mem_out.astype(jnp.bfloat16)
+    none = jnp.zeros_like(q_value)
+    right_value = jnp.concatenate([q_value, none], axis=1).astype(jnp.bfloat16)
+    right_out = jnp.concatenate([none, q_out], axis=1).astype(jnp.bfloat16)
+    part = jnp.dot(kept_value, right_value, preferred_element_type=jnp.float32)
+    part = part + lax.dot_general(
+        kept_out, right_out, (((0,), (0,)), ((), ())), preferred_element_type=jnp.float32
+    )
+    p_both = reduce_left(part.astype(jnp.bfloat16), replicas, depth)
+    gram = lax.dot_general(
+        p_both, p_both, (((0,), (0,)), ((), ())), preferred_element_type=jnp.float32
+    )
+    first = jnp.arange(2 * rank)[None, :] < rank
+    nothing = jnp.zeros_like(p_both)
+    term = lax.dot_general(
+        kept_value,
+        jnp.where(first, p_both, nothing),
+        (((0,), (0,)), ((), ())),
+        preferred_element_type=jnp.float32,
+    )
+    term = term + jnp.dot(
+        kept_out, jnp.where(first, nothing, p_both), preferred_element_type=jnp.float32
+    )
+    terms, low = reduce_right(term, gram, replicas)
+    phat = lax.dot_general(
+        p_both.astype(jnp.float32), low, (((1,), (1,)), ((), ())), precision=HIGH
+    )
     new_q = lax.dot_general(terms, low, (((1,), (1,)), ((), ())), precision=HIGHEST) / replicas
     new_q_value = new_q[:, :rank]
     new_q_out = new_q[:, rank:]
+    rough_phat = phat.astype(jnp.bfloat16)
+    rough_q = new_q.astype(jnp.bfloat16)
     full_value = lax.dot_general(
-        phat[:, :rank], new_q_value, (((1,), (1,)), ((), ())), precision=HIGH
+        rough_phat[:, :rank],
+        rough_q[:, :rank],
+        (((1,), (1,)), ((), ())),
+        preferred_element_type=jnp.float32,
     )
     full_out = lax.dot_general(
-        new_q_out, phat[:, rank:], (((1,), (1,)), ((), ())), precision=HIGH
+        rough_q[:, rank:],
+        rough_phat[:, rank:],
+        (((1,), (1,)), ((), ())),
+        preferred_element_type=jnp.float32,
     )
     new_err_value = (mem_value - full_value).astype(jnp.bfloat16)[None]
     new_err_out = (mem_out - full_out).astype(jnp.bfloat16)[None]

time: 165 us -> 168 us (1.018)
  Pallas kernels: 66.4 us -> 106 us
  waiting for transfers between devices: 14.4 us -> 0.01 us
  between operations: 15.1 us -> 1.77 us
  matrix products: 38.8 us -> 28.4 us
  local copies, waits for them, and re-layouts: 18.8 us -> 11.1 us
  starting transfers between devices: 0.04 us -> 6.06 us
  other arithmetic: 11.2 us -> 15.2 us
    pallas_call x1, Pallas kernels: 20.6 us -> 65.6 us  [gather_table(): pl.pallas_call(functools.partial(table_kernel, chips, depth), out_shape=(...]
    dot_general x8, matrix products: 25.6 us -> 11 us  [the longest x1 3.22 us: shards(): lax.dot_general(rough_q[:, rank:], rough_phat[:, rank:], (((1,), (1,)), (...]
    all_gather x1 -> x0, waiting for transfers between devices: 13.7 us -> none  [shards(): dy_whole = lax.all_gather(cotangent, 'mdl', axis=2, tiled=True)]
    unnamed x48 -> x26, local copies, waits for them, and re-layouts: 10.7 us -> 2.41 us
    dynamic_update_slice x0 -> x3, local copies, waits for them, and re-layouts: none -> 6.1 us  [shards(): dy_rows = lax.dynamic_update_slice(dy_rows, pieces[j], (0, source * width))]
    ppermute x0 -> x3, starting transfers between devices: none -> 6.06 us  [shards(): lax.ppermute(masked, 'mdl', [(i, (i + j) % depth) for i in range(depth)])]
    pallas_call x1, Pallas kernels: 30.3 us -> 25.1 us  [reduce_left(): pl.pallas_call(functools.partial(left_kernel, chips, depth), out_shape=ja...]
    another operation x1 -> x3, other arithmetic: 2.29 us -> 6.88 us
  transfers between devices with their start and end apart: 1 -> 3, of which waited for: 1 -> 0; matrix products, arithmetic and copies ran while one was open for 12% -> 14% of each run, Pallas kernels for 13% -> 39%
where the time goes in v2:
time: 168 us
  Pallas kernels  106 us (63%)
  matrix products  28.4 us (17%)
  other arithmetic  15.2 us (9%)
  local copies, waits for them, and re-layouts  11.1 us (7%)
  starting transfers between devices  6.06 us (4%)
  between operations  1.77 us (1%)
    pallas_call x1, Pallas kernels, gather_table(): pl.pallas_call(functools.partial(table_kernel, chips, depth), out_shape=(...  65.6 us
    pallas_call x1, Pallas kernels, reduce_left(): pl.pallas_call(functools.partial(left_kernel, chips, depth), out_shape=ja...  25.1 us
    pallas_call x1, Pallas kernels, reduce_right(): pl.pallas_call(functools.partial(right_kernel, chips, rank), out_shape=(j...  14.8 us
    another operation x3, other arithmetic  6.88 us
    dynamic_update_slice x3, local copies, waits for them, and re-layouts, shards(): dy_rows = lax.dynamic_update_slice(dy_rows, pieces[j], (0, source * width))  6.1 us
    ppermute x3, starting transfers between devices, shards(): lax.ppermute(masked, 'mdl', [(i, (i + j) % depth) for i in range(depth)])  6.06 us
    dot_general x1, matrix products, shards(): jnp.einsum('shqk,skhd->sqhd', weights, values4, preferred_element_type=jn...  3.73 us
    dot_general x1, matrix products, shards(): lax.dot_general(context, dy_rows, (((0,), (0,)), ((), ())), preferred_ele...  3.46 us
  transfers between devices with their start and end apart: 3, of which 0 were waited for; matrix products, arithmetic and copies ran while one was open for 14% of the time, Pallas kernels for 39%

profile of v2, /device:TPU:0, one launch (start us, length us, event | category | flops | bytes accessed | tf_op | source)
XLA Modules:
  0.0 168.1 jit_solution(17548568272260635960)
XLA Ops:
  1.5 1.7 broadcast_in_dim.66
  3.1 2.6 %constant_dynamic-update-slice_fusion.3 = (bf16[512,2560]{1,0:T(8,128)(2,1)}, bf16[512,640]{1,0:T(8,128)(2,1)S(1)}) fusion(bf16[512,2560]{1,0:T(8,128)(2,1)} %broadcast_in_dim.66, s32[]{:T(128)S(6)} %select_n.28, bf16[1,512,640]{2,1,0:T(8,128)(2,1)} %param.17, pred[512]{0:T(512)(128)(4,1)S(1)} %iota_compare_fusion.3), kind=kLoop, calls=%fused_computation.60 | loop fusion | flops 327680 | bytes 1966596 | tf_op jit(solution)/shard_map/dynamic_update_slice | solution.py:384
  5.8 5.0 %collective-permute-start.1 = (bf16[512,640]{1,0:T(8,128)(2,1)S(1)}, bf16[512,640]{1,0:T(8,128)(2,1)}, u32[]{:S(2)}, u32[]{:S(2)}) collective-permute-start(bf16[512,640]{1,0:T(8,128)(2,1)S(1)} %get-tuple-element.15), channel_id=1, source_target_pairs={{0,3},{1,0},{2,1},{3,2},{4,7},{5,4},{6,5},{7,6},{8,11},{9,8},{10,9... | collective-permute-start | bytes 1966088 | tf_op jit(solution)/shard_map/ppermute | solution.py:359
  10.8 1.0 collective-permute-start.2
  12.8 2.1 %fusion.1 = f32[8,512]{1,0:T(8,128)S(1)} fusion(bf16[1,8,512,512]{3,2,1,0:T(8,128)(2,1)S(1)} %copy-done.5, f32[8,512]{1,0:T(8,128)S(1)} %fusion, pred[512]{0:T(512)(128)(4,1)S(1)} %iota_compare_fusion.3), kind=kLoop, calls=%fused_computation.4 | loop fusion | flops 8384512 | bytes 4227584 | tf_op jit(solution)/shard_map/reduce_sum | solution.py:374
  14.9 65.6 %shard_map.163 = (bf16[8,48,2560]{2,1,0:T(8,128)(2,1)S(1)}, bf16[4,16,640]{2,1,0:T(8,128)(2,1)S(1)}) custom-call(bf16[8,48,640]{2,1,0:T(8,128)(2,1)S(1)} %bitcast.69, bf16[16,640]{1,0:T(8,128)(2,1)S(1)} %broadcast_in_dim.65.gain_ref), custom_call_target="tpu_custom_call" | custom-call | tf_op jit(solution)/shard_map/pallas_call | solution.py:117
  80.5 1.3 copy-done.1
  81.9 2.0 %multiply_reduce_fusion = f32[8,48]{1,0:T(8,128)S(1)} fusion(bf16[8,48,2560]{2,1,0:T(8,128)(2,1)} %copy-done.1), kind=kLoop, calls=%fused_computation.14 | loop fusion | flops 2948736 | bytes 1967616 | tf_op jit(solution)/shard_map/reduce_sum | solution.py:362
  84.0 5.0 %fusion.2 = bf16[8,512,512]{2,1,0:T(8,128)(2,1)} fusion(bf16[1,8,512,512]{3,2,1,0:T(8,128)(2,1)} %param.16, f32[8,512]{1,0:T(8,128)S(1)} %fusion.1, f32[8,512]{1,0:T(8,128)S(1)} %fusion, pred[512]{0:T(512)(128)(4,1)S(1)} %iota_compare_fusion.3), kind=kLoop, calls=%fused_computation.10 | loop fusion | flops 10485760 | bytes 8421888 | tf_op jit(solution)/shard_map/reshape.6
  89.7 1.6 convolution_convert_fusion
  91.3 2.4 %convolution_convert_fusion.4 = bf16[512,512]{0,1:T(8,128)(2,1)} fusion(bf16[512,2560]{1,0:T(8,128)(2,1)S(1)} %convolution_convert_fusion, bf16[2560,512]{1,0:T(8,128)(2,1)S(1)} %copy-done), kind=kOutput, calls=%fused_computation.29 | convolution fusion | flops 1342439424 | bytes 5767168 | tf_op jit(solution)/shard_map/dot_general | solution.py:370
  95.6 3.7 %convolution_convert_fusion.2 = bf16[8,64,512]{2,1,0:T(8,128)(2,1)S(1)} fusion(bf16[512,8,64]{0,2,1:T(8,128)(2,1)} %bitcast.73, bf16[8,512,512]{2,1,0:T(8,128)(2,1)} %fusion.2), kind=kOutput, calls=%fused_computation.27 | convolution fusion | flops 268697600 | bytes 5242880 | tf_op jit(solution)/shard_map/shqk,skhd->sqhd/dot_general | solution.py:377
  99.3 2.1 %constant_dynamic-update-slice_fusion.2 = bf16[512,2560]{1,0:T(8,128)(2,1)} fusion(bf16[512,2560]{1,0:T(8,128)(2,1)} %get-tuple-element.14, bf16[512,640]{1,0:T(8,128)(2,1)} %collective-permute-done, s32[]{:T(128)S(6)} %select_n.29), kind=kLoop, calls=%fused_computation.59 | loop fusion | bytes 1310724 | tf_op jit(solution)/shard_map/dynamic_update_slice | solution.py:384
  101.5 2.0 %constant_dynamic-update-slice_fusion.1 = bf16[512,2560]{1,0:T(8,128)(2,1)} fusion(bf16[512,2560]{1,0:T(8,128)(2,1)} %constant_dynamic-update-slice_fusion.2, bf16[512,640]{1,0:T(8,128)(2,1)} %collective-permute-done.1, s32[]{:T(128)S(6)} %select_n.30), kind=kLoop, calls=%fused_computation.58 | loop fusion | bytes 1310724 | tf_op jit(solution)/shard_map/dynamic_update_slice | solution.py:384
  103.4 2.0 %constant_dynamic-update-slice_fusion = bf16[512,2560]{1,0:T(8,128)(2,1)} fusion(bf16[512,2560]{1,0:T(8,128)(2,1)} %constant_dynamic-update-slice_fusion.1, bf16[512,640]{1,0:T(8,128)(2,1)} %collective-permute-done.2, s32[]{:T(128)S(6)} %select_n.31), kind=kLoop, calls=%fused_computation.57 | loop fusion | bytes 1310724 | tf_op jit(solution)/shard_map/dynamic_update_slice | solution.py:384
  105.4 3.4 %convolution_convert_fusion.5 = bf16[512,512]{0,1:T(8,128)(2,1)S(1)} fusion(bf16[512,2560]{1,0:T(8,128)(2,1)} %constant_dynamic-update-slice_fusion, bf16[512,2560]{1,0:T(8,128)(2,1)S(1)} %copy-done.11), kind=kOutput, calls=%fused_computation.30 | convolution fusion | flops 1342439424 | bytes 5767168 | tf_op jit(solution)/shard_map/dot_general | solution.py:385
  110.6 3.5 %convert_add_fusion = f32[512,2560]{1,0:T(8,128)S(1)} fusion(bf16[512,512]{0,1:T(8,128)(2,1)S(1)} %bitcast.72, bf16[512,2560]{1,0:T(8,128)(2,1)} %constant_dynamic-update-slice_fusion, bf16[1,512,2560]{2,1,0:T(8,128)(2,1)S(1)} %copy-done.9), kind=kOutput, calls=%fused_computation.5 | convolution fusion | flops 1344798720 | bytes 11010048 | tf_op jit(solution)/shard_map/dot_general | solution.py:394
  114.1 1.7 convert_add_fusion.1
  116.6 0.9 fusion.5
  117.5 25.1 %shard_map.164 = bf16[2,4,4,80,128]{4,3,2,1,0:T(8,128)(2,1)S(1)} custom-call(bf16[2,4,4,80,128]{4,3,2,1,0:T(8,128)(2,1)S(1)} %bitcast.67), custom_call_target="tpu_custom_call" | custom-call | tf_op jit(solution)/shard_map/pallas_call | solution.py:253
  143.9 1.1 fusion.15
  145.1 14.8 %shard_map.165 = (f32[2,4,1,64,128]{4,3,2,1,0:T(8,128)S(1)}, f32[128,128]{1,0:T(8,128)S(1)}) custom-call(f32[2,4,1,64,128]{4,3,2,1,0:T(8,128)S(1)} %bitcast.68, f32[128,128]{1,0:T(8,128)S(1)} %maximum_maximum_fusion.gram_ref), custom_call_target="tpu_custom_call" | custom-call | tf_op jit(solution)/shard_map/pallas_call | solution.py:314
  160.9 3.2 %fusion.7 = (bf16[1,512,2560]{2,1,0:T(8,128)(2,1)}, bf16[512,2560]{1,0:T(8,128)(2,1)}) fusion(f32[512,2560]{1,0:T(8,128)S(1)} %convert_add_fusion, bf16[2560,128]{0,1:T(8,128)(2,1)S(1)} %convolution_convert_fusion.1, bf16[512,128]{0,1:T(8,128)(2,1)S(1)} %get-tuple-element.24), kind=kOutput, calls=%fused_computation.19 | convolution fusion | flops 171704320 | bytes 10878976 | tf_op jit(solution)/shard_map/dot_general | solution.py:441
  164.1 3.2 %fusion.6 = (bf16[1,2560,512]{2,1,0:T(8,128)(2,1)}, bf16[2560,512]{1,0:T(8,128)(2,1)}) fusion(f32[2560,512]{1,0:T(8,128)S(1)} %convert_add_fusion.1, bf16[512,128]{0,1:T(8,128)(2,1)S(1)} %get-tuple-element.24, bf16[2560,128]{0,1:T(8,128)(2,1)S(1)} %convolution_convert_fusion.1), kind=kOutput, calls=%fused_computation.18 | convolution fusion | flops 171704320 | bytes 10878976 | tf_op jit(solution)/shard_map/dot_general | solution.py:435
  (50 shorter events, 9.2 us)
Async XLA Ops:
  0.6 90.6 %copy-start = (bf16[2560,512]{1,0:T(8,128)(2,1)S(1)}, bf16[2560,512]{1,0:T(8,128)(2,1)}, u32[]{:S(2)}) copy-start(bf16[2560,512]{1,0:T(8,128)(2,1)} %param.18) | copy-start | bytes 7864324
  1.5 10.4 %copy-start.5 = (bf16[1,8,512,512]{3,2,1,0:T(8,128)(2,1)S(1)}, bf16[1,8,512,512]{3,2,1,0:T(8,128)(2,1)}, u32[]{:S(2)}) copy-start(bf16[1,8,512,512]{3,2,1,0:T(8,128)(2,1)} %param.16) | copy-start | bytes 12582916
  5.8 95.7 %collective-permute-start.1 = (bf16[512,640]{1,0:T(8,128)(2,1)S(1)}, bf16[512,640]{1,0:T(8,128)(2,1)}, u32[]{:S(2)}, u32[]{:S(2)}) collective-permute-start(bf16[512,640]{1,0:T(8,128)(2,1)S(1)} %get-tuple-element.15), channel_id=1, source_target_pairs={{0,3},{1,0},{2,1},{3,2},{4,7},{5,4},{6,5},{7,6},{8,11},{9,8},{10,9... | collective-permute-start | bytes 1966088 | tf_op jit(solution)/shard_map/ppermute | solution.py:359
  10.8 88.5 %collective-permute-start = (bf16[512,640]{1,0:T(8,128)(2,1)S(1)}, bf16[512,640]{1,0:T(8,128)(2,1)}, u32[]{:S(2)}, u32[]{:S(2)}) collective-permute-start(bf16[512,640]{1,0:T(8,128)(2,1)S(1)} %get-tuple-element.15), channel_id=1, source_target_pairs={{0,1},{1,2},{2,3},{3,0},{4,5},{5,6},{6,7},{7,4},{8,9},{9,10},{10,1... | collective-permute-start | bytes 1966088 | tf_op jit(solution)/shard_map/ppermute | solution.py:359
  10.8 92.6 %collective-permute-start.2 = (bf16[512,640]{1,0:T(8,128)(2,1)S(1)}, bf16[512,640]{1,0:T(8,128)(2,1)}, u32[]{:S(2)}, u32[]{:S(2)}) collective-permute-start(bf16[512,640]{1,0:T(8,128)(2,1)S(1)} %get-tuple-element.15), channel_id=1, source_target_pairs={{0,2},{1,3},{2,0},{3,1},{4,6},{5,7},{6,4},{7,5},{8,10},{9,11},{10,... | collective-permute-start | bytes 1966088 | tf_op jit(solution)/shard_map/ppermute | solution.py:359
  12.8 2.1 %copy-start.10 = (bf16[640]{0:T(1024)(128)(2,1)S(1)}, bf16[640]{0:T(1024)(128)(2,1)}, u32[]{:S(2)}) copy-start(bf16[640]{0:T(1024)(128)(2,1)} %param.15) | copy-start | bytes 3844
  12.8 2.1 %copy-start.3 = (bf16[384,640]{1,0:T(8,128)(2,1)S(1)}, bf16[384,640]{1,0:T(8,128)(2,1)}, u32[]{:S(2)}) copy-start(bf16[384,640]{1,0:T(8,128)(2,1)} %param.14) | copy-start | bytes 1474564
  80.5 1.3 copy-start.1
  84.0 5.1 %copy-start.2 = (bf16[8,48,2560]{2,1,0:T(8,128)(2,1)S(1)}, bf16[8,48,2560]{2,1,0:T(8,128)(2,1)}, u32[]{:S(2)}) copy-start(bf16[8,48,2560]{2,1,0:T(8,128)(2,1)} %copy-done.1) | copy-start | bytes 5898244
  89.0 0.7 copy-start.12
  91.3 2.4 %copy-start.7 = (bf16[512,2560]{1,0:T(8,128)(2,1)}, bf16[512,2560]{1,0:T(8,128)(2,1)S(1)}, u32[]{:S(2)}) copy-start(bf16[512,2560]{1,0:T(8,128)(2,1)S(1)} %convolution_convert_fusion) | copy-start | bytes 7864324
  99.3 6.1 %copy-start.11 = (bf16[512,2560]{1,0:T(8,128)(2,1)S(1)}, bf16[512,2560]{1,0:T(8,128)(2,1)}, u32[]{:S(2)}) copy-start(bf16[512,2560]{1,0:T(8,128)(2,1)} %param.19) | copy-start | bytes 7864324
  105.4 3.4 %copy-start.4 = (bf16[8,512,512]{2,1,0:T(8,128)(2,1)S(1)}, bf16[8,512,512]{2,1,0:T(8,128)(2,1)}, u32[]{:S(2)}) copy-start(bf16[8,512,512]{2,1,0:T(8,128)(2,1)} %fusion.2) | copy-start | bytes 12582916
  108.9 1.7 %copy-start.9 = (bf16[1,512,2560]{2,1,0:T(8,128)(2,1)S(1)}, bf16[1,512,2560]{2,1,0:T(8,128)(2,1)}, u32[]{:S(2)}) copy-start(bf16[1,512,2560]{2,1,0:T(8,128)(2,1)} %param.21) | copy-start | bytes 7864324
  110.6 3.5 %copy-start.6 = (bf16[1,2560,512]{2,1,0:T(8,128)(2,1)S(1)}, bf16[1,2560,512]{2,1,0:T(8,128)(2,1)}, u32[]{:S(2)}) copy-start(bf16[1,2560,512]{2,1,0:T(8,128)(2,1)} %param.20) | copy-start | bytes 7864324
  110.6 3.5 %copy-start.8 = (bf16[512,2560]{1,0:T(8,128)(2,1)S(1)}, bf16[512,2560]{1,0:T(8,128)(2,1)}, u32[]{:S(2)}) copy-start(bf16[512,2560]{1,0:T(8,128)(2,1)} %copy-done.7) | copy-start | bytes 7864324

commit v3 on v2

--- a/solution.py
+++ b/solution.py
@@ -349,14 +349,8 @@
     vocab = embedding.shape[0]
     rows = samples * seq
     rank = q_value.shape[1]
-    spot = lax.axis_index("mdl")
-    live = jnp.arange(seq, dtype=jnp.int32)[None, :] < lengths[:, None]
-    masked = jnp.where(live[..., None], cotangent, jnp.zeros_like(cotangent)).reshape(rows, -1)
-    width = masked.shape[1]
-    width_full = width * depth
-    pieces = [masked]
-    for j in range(1, depth):
-        pieces.append(lax.ppermute(masked, "mdl", [(i, (i + j) % depth) for i in range(depth)]))
+    dy_whole = lax.all_gather(cotangent, "mdl", axis=2, tiled=True)
+    width_full = dy_whole.shape[2]
     raw, gain = gather_table(embedding, norm_gain, replicas, depth)
     raw = raw.astype(jnp.float32)
     scale = lax.rsqrt(jnp.sum(raw * raw, axis=1) / width_full + 1e-06)
@@ -364,6 +358,7 @@
     flat_ids = token_ids.reshape(rows)
     onehot = (flat_ids[:, None] == jnp.arange(vocab, dtype=jnp.int32)[None, :]).astype(jnp.bfloat16)
     normed = jnp.dot(onehot, table, preferred_element_type=jnp.float32).astype(jnp.bfloat16)
+    live = jnp.arange(seq, dtype=jnp.int32)[None, :] < lengths[:, None]
     heads_local = scores.shape[1]
     inner_local = w_value.shape[1]
     head_size = inner_local // heads_local
@@ -378,10 +373,9 @@
         .astype(jnp.bfloat16)
         .reshape(rows, inner_local)
     )
-    dy_rows = jnp.zeros((rows, width_full), jnp.bfloat16)
-    for j in (0, 1, 3, 2) if depth == 4 else range(depth):
-        source = lax.rem(spot - j + depth, depth)
-        dy_rows = lax.dynamic_update_slice(dy_rows, pieces[j], (0, source * width))
+    dy_rows = jnp.where(live[..., None], dy_whole, jnp.zeros_like(dy_whole)).reshape(
+        rows, width_full
+    )
     dcontext = lax.dot_general(
         dy_rows, w_out, (((1,), (1,)), ((), ())), preferred_element_type=jnp.float32
     ).astype(jnp.bfloat16)

time: 168 us -> 139 us (0.83)
  Pallas kernels: 106 us -> 58.9 us
  waiting for transfers between devices: 0.01 us -> 19.2 us
  between operations: 1.77 us -> 15 us
  starting transfers between devices: 6.06 us -> 0.04 us
  matrix products: 28.4 us -> 24 us
  other arithmetic: 15.2 us -> 11.4 us
    pallas_call x1, Pallas kernels: 65.6 us -> 20.4 us  [gather_table(): pl.pallas_call(functools.partial(table_kernel, chips, depth), out_shape=(...]
    all_gather x0 -> x1, waiting for transfers between devices: none -> 18.5 us  [shards(): dy_whole = lax.all_gather(cotangent, 'mdl', axis=2, tiled=True)]
    dynamic_update_slice x3 -> x0, local copies, waits for them, and re-layouts: 6.1 us -> none  [shards(): dy_rows = lax.dynamic_update_slice(dy_rows, pieces[j], (0, source * width))]
    ppermute x3 -> x0, starting transfers between devices: 6.06 us -> none  [shards(): lax.ppermute(masked, 'mdl', [(i, (i + j) % depth) for i in range(depth)])]
    unnamed x26 -> x24, local copies, waits for them, and re-layouts: 2.41 us -> 8.26 us
    another operation x3, other arithmetic: 6.88 us -> 4.13 us
    dynamic_update_slice x1 -> x0, other arithmetic: 2.64 us -> none  [shards(): dy_rows = lax.dynamic_update_slice(dy_rows, pieces[j], (0, source * width))]
    dot_general x1, matrix products: 3.73 us -> 1.37 us  [shards(): jnp.einsum('shqk,skhd->sqhd', weights, values4, preferred_element_type=jn...]
  transfers between devices with their start and end apart: 3 -> 1, of which waited for: 0 -> 1; matrix products, arithmetic and copies ran while one was open for 14% -> 12% of each run, Pallas kernels for 39% -> 15%
where the time goes in v3:
time: 139 us; the launch traced here: 138 us
  Pallas kernels  58.9 us (42%)
  matrix products  24 us (17%)
  waiting for transfers between devices  19.2 us (14%)
  between operations  15 us (11%)
  other arithmetic  11.4 us (8%)
  local copies, waits for them, and re-layouts  9.83 us (7%)
    pallas_call x1, Pallas kernels, reduce_left(): pl.pallas_call(functools.partial(left_kernel, chips, depth), out_shape=ja...  23.1 us
    pallas_call x1, Pallas kernels, gather_table(): pl.pallas_call(functools.partial(table_kernel, chips, depth), out_shape=(...  20.4 us
    all_gather x1, waiting for transfers between devices, shards(): dy_whole = lax.all_gather(cotangent, 'mdl', axis=2, tiled=True)  18.5 us
    pallas_call x1, Pallas kernels, reduce_right(): pl.pallas_call(functools.partial(right_kernel, chips, rank), out_shape=(j...  15.4 us
    unnamed x24, local copies, waits for them, and re-layouts  8.26 us
    dot_general x1, matrix products, shards(): lax.dot_general(dy_rows, w_out, (((1,), (1,)), ((), ())), preferred_eleme...  4.3 us
    another operation x3, other arithmetic  4.13 us
    dot_general x1, matrix products, shards(): lax.dot_general(rough_phat[:, :rank], rough_q[:, :rank], (((1,), (1,)), (...  3.22 us
  transfers between devices with their start and end apart: 1, of which 1 were waited for; matrix products, arithmetic and copies ran while one was open for 12% of the time, Pallas kernels for 15%

profile of v3, /device:TPU:0, one launch (start us, length us, event | category | flops | bytes accessed | tf_op | source)
XLA Modules:
  0.0 138.3 jit_solution(15981854209793582234)
XLA Ops:
  8.6 0.9 convert.12
  9.6 0.9 convert.13
  11.2 1.0 copy-done.2
  12.2 20.4 %shard_map.163 = (bf16[8,48,2560]{2,1,0:T(8,128)(2,1)S(1)}, bf16[4,16,640]{2,1,0:T(8,128)(2,1)S(1)}) custom-call(bf16[8,48,640]{2,1,0:T(8,128)(2,1)S(1)} %bitcast.71, bf16[16,640]{1,0:T(8,128)(2,1)S(1)} %broadcast_in_dim.62.gain_ref), custom_call_target="tpu_custom_call" | custom-call | tf_op jit(solution)/shard_map/pallas_call | solution.py:117
  32.6 1.3 copy-done.1
  33.9 2.0 %multiply_reduce_fusion = f32[8,48]{1,0:T(8,128)S(1)} fusion(bf16[8,48,2560]{2,1,0:T(8,128)(2,1)} %copy-done.1), kind=kLoop, calls=%fused_computation.14 | loop fusion | flops 2948736 | bytes 1967616 | tf_op jit(solution)/shard_map/reduce_sum | solution.py:356
  36.0 2.1 %fusion.4 = bf16[384,2560]{1,0:T(8,128)(2,1)S(1)} fusion(f32[2560]{0:T(1024)S(1)} %reshape.128, f32[384]{0:T(512)S(1)} %rsqrt.11, bf16[8,48,2560]{2,1,0:T(8,128)(2,1)} %copy-done.1), kind=kLoop, calls=%fused_computation.13 | loop fusion | flops 3932160 | bytes 3943936 | tf_op jit(solution)/shard_map/convert_element_type | solution.py:357
  38.1 1.6 %convolution_convert_fusion = bf16[512,2560]{1,0:T(8,128)(2,1)S(1)} fusion(bf16[384,2560]{1,0:T(8,128)(2,1)S(1)} %fusion.4, s32[512]{0:T(512)S(1)} %bitcast.77), kind=kOutput, calls=%fused_computation.9 | convolution fusion | flops 1008140288 | bytes 4589568 | tf_op jit(solution)/shard_map/dot_general | solution.py:360
  40.3 0.9 fusion
  41.2 1.6 %convolution_convert_fusion.4 = bf16[512,512]{0,1:T(8,128)(2,1)S(1)} fusion(bf16[512,2560]{1,0:T(8,128)(2,1)S(1)} %convolution_convert_fusion, bf16[2560,512]{1,0:T(8,128)(2,1)S(1)} %copy-done), kind=kOutput, calls=%fused_computation.34 | convolution fusion | flops 1342439424 | bytes 5767168 | tf_op jit(solution)/shard_map/dot_general | solution.py:365
  42.8 2.1 %fusion.1 = f32[8,512]{1,0:T(8,128)S(1)} fusion(bf16[1,8,512,512]{3,2,1,0:T(8,128)(2,1)S(1)} %copy-done.5, f32[8,512]{1,0:T(8,128)S(1)} %fusion, pred[512]{0:T(512)(128)(4,1)S(1)} %iota_compare_fusion.3), kind=kLoop, calls=%fused_computation.4 | loop fusion | flops 8384512 | bytes 4227584 | tf_op jit(solution)/shard_map/reduce_sum | solution.py:369
  44.9 2.3 %fusion.2 = bf16[8,512,512]{2,1,0:T(8,128)(2,1)S(1)} fusion(bf16[1,8,512,512]{3,2,1,0:T(8,128)(2,1)S(1)} %copy-done.5, f32[8,512]{1,0:T(8,128)S(1)} %fusion.1, f32[8,512]{1,0:T(8,128)S(1)} %fusion, pred[512]{0:T(512)(128)(4,1)S(1)} %iota_compare_fusion.3), kind=kLoop, calls=%fused_computation.10 | loop fusion | flops 10485760 | bytes 8421888 | tf_op jit(solution)/shard_map/reshape.6
  47.2 1.9 %copy-done.3 = bf16[8,512,512]{2,1,0:T(8,128)(2,1)} copy-done((bf16[8,512,512]{2,1,0:T(8,128)(2,1)}, bf16[8,512,512]{2,1,0:T(8,128)(2,1)S(1)}, u32[]{:S(2)}) %copy-start.3) | copy-done | bytes 4194328
  49.2 1.4 convolution_convert_fusion.2
  50.5 18.5 %all-gather.2.cloned.1.call-done = bf16[1,512,2560]{2,1,0:T(8,128)(2,1)} async-done(((bf16[1,512,640]{2,1,0:T(8,128)(2,1)}), bf16[1,512,2560]{2,1,0:T(8,128)(2,1)}) %all-gather.2.cloned.1.call-update) | async-done | bytes 2621456 | tf_op jit(solution)/shard_map/all_gather | solution.py:352
  69.1 4.3 %fusion.18 = bf16[512,512]{0,1:T(8,128)(2,1)S(1)} fusion(bf16[512,2560]{1,0:T(8,128)(2,1)} %param.19, bf16[1,512,2560]{2,1,0:T(8,128)(2,1)} %all-gather.2.cloned.1.call-done, pred[512]{0:T(512)(128)(4,1)S(1)} %iota_compare_fusion.3), kind=kOutput, calls=%fused_computation.33 | convolution fusion | flops 1343750144 | bytes 5767680 | tf_op jit(solution)/shard_map/dot_general | solution.py:379
  74.2 0.9 copy-done.6
  75.9 1.6 %convert_add_fusion.1 = f32[2560,512]{1,0:T(8,128)S(1)} fusion(bf16[512,2560]{1,0:T(8,128)(2,1)S(1)} %copy-done.8, bf16[512,512]{0,1:T(8,128)(2,1)S(1)} %bitcast.74, bf16[1,2560,512]{2,1,0:T(8,128)(2,1)S(1)} %copy-done.6), kind=kOutput, calls=%fused_computation.6 | convolution fusion | flops 1344798720 | bytes 11010048 | tf_op jit(solution)/shard_map/dot_general | solution.py:391
  80.0 1.6 %convert_add_fusion = f32[512,2560]{1,0:T(8,128)S(1)} fusion(bf16[512,512]{0,1:T(8,128)(2,1)S(1)} %bitcast.73, bf16[1,512,2560]{2,1,0:T(8,128)(2,1)S(1)} %copy-done.9, bf16[1,512,2560]{2,1,0:T(8,128)(2,1)S(1)} %copy-done.10, pred[512]{0:T(512)(128)(4,1)S(1)} %iota_compare_fusion.3), kind=kOutput, calls=%fused_computation.5 | convolution fusion | flops 1346109440 | bytes 11010560 | tf_op jit(solution)/shard_map/dot_general | solution.py:388
  81.7 0.9 fusion.5
  82.6 23.1 %shard_map.164 = bf16[2,4,4,80,128]{4,3,2,1,0:T(8,128)(2,1)S(1)} custom-call(bf16[2,4,4,80,128]{4,3,2,1,0:T(8,128)(2,1)S(1)} %bitcast.69), custom_call_target="tpu_custom_call" | custom-call | tf_op jit(solution)/shard_map/pallas_call | solution.py:253
  108.0 15.4 %shard_map.165 = (f32[2,4,1,64,128]{4,3,2,1,0:T(8,128)S(1)}, f32[128,128]{1,0:T(8,128)S(1)}) custom-call(f32[2,4,1,64,128]{4,3,2,1,0:T(8,128)S(1)} %bitcast.70, f32[128,128]{1,0:T(8,128)S(1)} %maximum_maximum_fusion.gram_ref), custom_call_target="tpu_custom_call" | custom-call | tf_op jit(solution)/shard_map/pallas_call | solution.py:314
  124.3 3.2 %fusion.7 = (bf16[1,512,2560]{2,1,0:T(8,128)(2,1)}, bf16[512,2560]{1,0:T(8,128)(2,1)}) fusion(f32[512,2560]{1,0:T(8,128)S(1)} %convert_add_fusion, bf16[2560,128]{0,1:T(8,128)(2,1)S(1)} %convolution_convert_fusion.1, bf16[512,128]{0,1:T(8,128)(2,1)S(1)} %get-tuple-element.22), kind=kOutput, calls=%fused_computation.19 | convolution fusion | flops 171704320 | bytes 10878976 | tf_op jit(solution)/shard_map/dot_general | solution.py:435
  127.5 3.2 %fusion.6 = (bf16[1,2560,512]{2,1,0:T(8,128)(2,1)}, bf16[2560,512]{1,0:T(8,128)(2,1)}) fusion(f32[2560,512]{1,0:T(8,128)S(1)} %convert_add_fusion.1, bf16[512,128]{0,1:T(8,128)(2,1)S(1)} %get-tuple-element.22, bf16[2560,128]{0,1:T(8,128)(2,1)S(1)} %convolution_convert_fusion.1), kind=kOutput, calls=%fused_computation.18 | convolution fusion | flops 171704320 | bytes 10878976 | tf_op jit(solution)/shard_map/dot_general | solution.py:429
  (40 shorter events, 10.2 us)
Async XLA Ops:
  7.2 34.0 %copy-start = (bf16[2560,512]{1,0:T(8,128)(2,1)S(1)}, bf16[2560,512]{1,0:T(8,128)(2,1)}, u32[]{:S(2)}) copy-start(bf16[2560,512]{1,0:T(8,128)(2,1)} %param.18) | copy-start | bytes 7864324
  7.2 61.9 %all-gather.2.cloned.1.call-start = ((), (), s32[]{:S(2)}) async-start(), calls=%async_computation | async-start | bytes 3276800 | tf_op jit(solution)/shard_map/all_gather | solution.py:352
  11.2 1.0 copy-start.2
  32.6 1.3 copy-start.1
  33.9 4.2 %copy-start.11 = (s32[1,512]{1,0:T(1,128)S(1)}, s32[1,512]{1,0:T(1,128)}, u32[]{:S(2)}) copy-start(s32[1,512]{1,0:T(1,128)} %param.12) | copy-start | bytes 6148
  38.1 2.2 %copy-start.5 = (bf16[1,8,512,512]{3,2,1,0:T(8,128)(2,1)S(1)}, bf16[1,8,512,512]{3,2,1,0:T(8,128)(2,1)}, u32[]{:S(2)}) copy-start(bf16[1,8,512,512]{3,2,1,0:T(8,128)(2,1)} %param.16) | copy-start | bytes 12582916
  40.3 2.5 %copy-start.7 = (bf16[512,2560]{1,0:T(8,128)(2,1)}, bf16[512,2560]{1,0:T(8,128)(2,1)S(1)}, u32[]{:S(2)}) copy-start(bf16[512,2560]{1,0:T(8,128)(2,1)S(1)} %convolution_convert_fusion) | copy-start | bytes 7864324
  47.2 1.9 %copy-start.3 = (bf16[8,512,512]{2,1,0:T(8,128)(2,1)}, bf16[8,512,512]{2,1,0:T(8,128)(2,1)S(1)}, u32[]{:S(2)}) copy-start(bf16[8,512,512]{2,1,0:T(8,128)(2,1)S(1)} %fusion.2) | copy-start | bytes 12582916
  69.1 4.3 %copy-start.4 = (bf16[8,512,512]{2,1,0:T(8,128)(2,1)S(1)}, bf16[8,512,512]{2,1,0:T(8,128)(2,1)}, u32[]{:S(2)}) copy-start(bf16[8,512,512]{2,1,0:T(8,128)(2,1)} %copy-done.3) | copy-start | bytes 12582916
  73.4 1.7 %copy-start.6 = (bf16[1,2560,512]{2,1,0:T(8,128)(2,1)S(1)}, bf16[1,2560,512]{2,1,0:T(8,128)(2,1)}, u32[]{:S(2)}) copy-start(bf16[1,2560,512]{2,1,0:T(8,128)(2,1)} %param.20) | copy-start | bytes 7864324
  73.4 2.5 %copy-start.8 = (bf16[512,2560]{1,0:T(8,128)(2,1)S(1)}, bf16[512,2560]{1,0:T(8,128)(2,1)}, u32[]{:S(2)}) copy-start(bf16[512,2560]{1,0:T(8,128)(2,1)} %copy-done.7) | copy-start | bytes 7864324
  77.5 1.7 %copy-start.9 = (bf16[1,512,2560]{2,1,0:T(8,128)(2,1)S(1)}, bf16[1,512,2560]{2,1,0:T(8,128)(2,1)}, u32[]{:S(2)}) copy-start(bf16[1,512,2560]{2,1,0:T(8,128)(2,1)} %param.21) | copy-start | bytes 7864324
  77.5 2.5 %copy-start.10 = (bf16[1,512,2560]{2,1,0:T(8,128)(2,1)S(1)}, bf16[1,512,2560]{2,1,0:T(8,128)(2,1)}, u32[]{:S(2)}) copy-start(bf16[1,512,2560]{2,1,0:T(8,128)(2,1)} %all-gather.2.cloned.1.call-done) | copy-start | bytes 7864324
Sparse Core Ops, SparseCore 0:
  9.6 59.3 all-gather.1

commit v4 on v3

--- a/solution.py
+++ b/solution.py
@@ -271,15 +271,16 @@
         for h in range(2):
             lane = j + (rank if h == 0 else 0)
             part = tiles[h]
-            pivot = part[at][line : line + 1, lane : lane + 1]
-            inverse = 1.0 / jnp.sqrt(pivot)
-            row = part[at][line : line + 1, :] * inverse
+            row = part[at][line : line + 1, :]
+            columns = [
+                jnp.broadcast_to(part[t][:, lane : lane + 1], (8, 128))
+                for t in range(at, rank // 8)
+            ]
+            scaled = row * (1.0 / columns[0][line : line + 1, :])
             for t in range(at, rank // 8):
-                tile = part[t]
-                column = tile[:, lane : lane + 1] * inverse
-                fresh = tile - column * row
+                fresh = part[t] - columns[t - at] * scaled
                 if t == at:
-                    fresh = jnp.where(lines > line, fresh, jnp.where(lines == line, row, tile))
+                    fresh = jnp.where(lines > line, fresh, part[t])
                 part[t] = fresh
     for h in range(2):
         for t in range(rank // 8):
@@ -294,8 +295,13 @@
 
     reduce_steps(chips, 1, p_ref, out_ref, b1, b2, b3, sems, between)
     lanes = lax.broadcasted_iota(jnp.int32, (rank, 128), 1)
-    low_ref[:rank, :] = jnp.where(lanes < rank, work[:rank, :], 0.0)
-    low_ref[rank:, :] = jnp.where(lanes >= rank, work[rank:, :], 0.0)
+    lines = lax.broadcasted_iota(jnp.int32, (rank, 128), 0)
+    top = work[:rank, :]
+    pivots = jnp.sum(jnp.where(lanes == lines + rank, top, 0.0), axis=1, keepdims=True)
+    low_ref[:rank, :] = jnp.where(lanes < rank, top / jnp.sqrt(pivots), 0.0)
+    end = work[rank:, :]
+    pivots = jnp.sum(jnp.where(lanes == lines, end, 0.0), axis=1, keepdims=True)
+    low_ref[rank:, :] = jnp.where(lanes >= rank, end / jnp.sqrt(pivots), 0.0)
 
 
 def reduce_right(p, gram, replicas):

time: 139 us -> 138 us (level)
  no operation moved by 1% of the time
where the time goes in v4:
time: 138 us; the launch traced here: 137 us
  Pallas kernels  58 us (42%)
  matrix products  24 us (17%)
  waiting for transfers between devices  19.2 us (14%)
  between operations  15 us (11%)
  other arithmetic  11.4 us (8%)
  local copies, waits for them, and re-layouts  9.83 us (7%)
    pallas_call x1, Pallas kernels, reduce_left(): pl.pallas_call(functools.partial(left_kernel, chips, depth), out_shape=ja...  23.1 us
    pallas_call x1, Pallas kernels, gather_table(): pl.pallas_call(functools.partial(table_kernel, chips, depth), out_shape=(...  20.4 us
    all_gather x1, waiting for transfers between devices, shards(): dy_whole = lax.all_gather(cotangent, 'mdl', axis=2, tiled=True)  18.5 us
    pallas_call x1, Pallas kernels, reduce_right(): pl.pallas_call(functools.partial(right_kernel, chips, rank), out_shape=(j...  14.5 us
    unnamed x24, local copies, waits for them, and re-layouts  8.26 us
    dot_general x1, matrix products, shards(): lax.dot_general(dy_rows, w_out, (((1,), (1,)), ((), ())), preferred_eleme...  4.3 us
    another operation x3, other arithmetic  4.13 us
    dot_general x1, matrix products, shards(): lax.dot_general(rough_phat[:, :rank], rough_q[:, :rank], (((1,), (1,)), (...  3.22 us
  transfers between devices with their start and end apart: 1, of which 1 were waited for; matrix products, arithmetic and copies ran while one was open for 12% of the time, Pallas kernels for 15%

profile of v4, /device:TPU:0, one launch (start us, length us, event | category | flops | bytes accessed | tf_op | source)
XLA Modules:
  0.0 137.4 jit_solution(2285717313827276181)
XLA Ops:
  8.6 0.9 convert.12
  9.6 0.9 convert.13
  11.2 1.0 copy-done.2
  12.2 20.4 %shard_map.163 = (bf16[8,48,2560]{2,1,0:T(8,128)(2,1)S(1)}, bf16[4,16,640]{2,1,0:T(8,128)(2,1)S(1)}) custom-call(bf16[8,48,640]{2,1,0:T(8,128)(2,1)S(1)} %bitcast.71, bf16[16,640]{1,0:T(8,128)(2,1)S(1)} %broadcast_in_dim.62.gain_ref), custom_call_target="tpu_custom_call" | custom-call | tf_op jit(solution)/shard_map/pallas_call | solution.py:117
  32.6 1.3 copy-done.1
  33.9 2.0 %multiply_reduce_fusion = f32[8,48]{1,0:T(8,128)S(1)} fusion(bf16[8,48,2560]{2,1,0:T(8,128)(2,1)} %copy-done.1), kind=kLoop, calls=%fused_computation.14 | loop fusion | flops 2948736 | bytes 1967616 | tf_op jit(solution)/shard_map/reduce_sum | solution.py:362
  36.0 2.1 %fusion.4 = bf16[384,2560]{1,0:T(8,128)(2,1)S(1)} fusion(f32[2560]{0:T(1024)S(1)} %reshape.128, f32[384]{0:T(512)S(1)} %rsqrt.11, bf16[8,48,2560]{2,1,0:T(8,128)(2,1)} %copy-done.1), kind=kLoop, calls=%fused_computation.13 | loop fusion | flops 3932160 | bytes 3943936 | tf_op jit(solution)/shard_map/convert_element_type | solution.py:363
  38.1 1.6 %convolution_convert_fusion = bf16[512,2560]{1,0:T(8,128)(2,1)S(1)} fusion(bf16[384,2560]{1,0:T(8,128)(2,1)S(1)} %fusion.4, s32[512]{0:T(512)S(1)} %bitcast.77), kind=kOutput, calls=%fused_computation.9 | convolution fusion | flops 1008140288 | bytes 4589568 | tf_op jit(solution)/shard_map/dot_general | solution.py:366
  40.3 0.9 fusion
  41.2 1.6 %convolution_convert_fusion.4 = bf16[512,512]{0,1:T(8,128)(2,1)S(1)} fusion(bf16[512,2560]{1,0:T(8,128)(2,1)S(1)} %convolution_convert_fusion, bf16[2560,512]{1,0:T(8,128)(2,1)S(1)} %copy-done), kind=kOutput, calls=%fused_computation.34 | convolution fusion | flops 1342439424 | bytes 5767168 | tf_op jit(solution)/shard_map/dot_general | solution.py:371
  42.8 2.1 %fusion.1 = f32[8,512]{1,0:T(8,128)S(1)} fusion(bf16[1,8,512,512]{3,2,1,0:T(8,128)(2,1)S(1)} %copy-done.5, f32[8,512]{1,0:T(8,128)S(1)} %fusion, pred[512]{0:T(512)(128)(4,1)S(1)} %iota_compare_fusion.3), kind=kLoop, calls=%fused_computation.4 | loop fusion | flops 8384512 | bytes 4227584 | tf_op jit(solution)/shard_map/reduce_sum | solution.py:375
  44.9 2.3 %fusion.2 = bf16[8,512,512]{2,1,0:T(8,128)(2,1)S(1)} fusion(bf16[1,8,512,512]{3,2,1,0:T(8,128)(2,1)S(1)} %copy-done.5, f32[8,512]{1,0:T(8,128)S(1)} %fusion.1, f32[8,512]{1,0:T(8,128)S(1)} %fusion, pred[512]{0:T(512)(128)(4,1)S(1)} %iota_compare_fusion.3), kind=kLoop, calls=%fused_computation.10 | loop fusion | flops 10485760 | bytes 8421888 | tf_op jit(solution)/shard_map/reshape.6
  47.2 1.9 %copy-done.3 = bf16[8,512,512]{2,1,0:T(8,128)(2,1)} copy-done((bf16[8,512,512]{2,1,0:T(8,128)(2,1)}, bf16[8,512,512]{2,1,0:T(8,128)(2,1)S(1)}, u32[]{:S(2)}) %copy-start.3) | copy-done | bytes 4194328
  49.2 1.4 convolution_convert_fusion.2
  50.5 18.5 %all-gather.2.cloned.1.call-done = bf16[1,512,2560]{2,1,0:T(8,128)(2,1)} async-done(((bf16[1,512,640]{2,1,0:T(8,128)(2,1)}), bf16[1,512,2560]{2,1,0:T(8,128)(2,1)}) %all-gather.2.cloned.1.call-update) | async-done | bytes 2621456 | tf_op jit(solution)/shard_map/all_gather | solution.py:358
  69.1 4.3 %fusion.18 = bf16[512,512]{0,1:T(8,128)(2,1)S(1)} fusion(bf16[512,2560]{1,0:T(8,128)(2,1)} %param.19, bf16[1,512,2560]{2,1,0:T(8,128)(2,1)} %all-gather.2.cloned.1.call-done, pred[512]{0:T(512)(128)(4,1)S(1)} %iota_compare_fusion.3), kind=kOutput, calls=%fused_computation.33 | convolution fusion | flops 1343750144 | bytes 5767680 | tf_op jit(solution)/shard_map/dot_general | solution.py:385
  74.2 0.9 copy-done.6
  75.9 1.6 %convert_add_fusion.1 = f32[2560,512]{1,0:T(8,128)S(1)} fusion(bf16[512,2560]{1,0:T(8,128)(2,1)S(1)} %copy-done.8, bf16[512,512]{0,1:T(8,128)(2,1)S(1)} %bitcast.74, bf16[1,2560,512]{2,1,0:T(8,128)(2,1)S(1)} %copy-done.6), kind=kOutput, calls=%fused_computation.6 | convolution fusion | flops 1344798720 | bytes 11010048 | tf_op jit(solution)/shard_map/dot_general | solution.py:397
  80.0 1.6 %convert_add_fusion = f32[512,2560]{1,0:T(8,128)S(1)} fusion(bf16[512,512]{0,1:T(8,128)(2,1)S(1)} %bitcast.73, bf16[1,512,2560]{2,1,0:T(8,128)(2,1)S(1)} %copy-done.9, bf16[1,512,2560]{2,1,0:T(8,128)(2,1)S(1)} %copy-done.10, pred[512]{0:T(512)(128)(4,1)S(1)} %iota_compare_fusion.3), kind=kOutput, calls=%fused_computation.5 | convolution fusion | flops 1346109440 | bytes 11010560 | tf_op jit(solution)/shard_map/dot_general | solution.py:394
  81.7 0.9 fusion.5
  82.6 23.1 %shard_map.164 = bf16[2,4,4,80,128]{4,3,2,1,0:T(8,128)(2,1)S(1)} custom-call(bf16[2,4,4,80,128]{4,3,2,1,0:T(8,128)(2,1)S(1)} %bitcast.69), custom_call_target="tpu_custom_call" | custom-call | tf_op jit(solution)/shard_map/pallas_call | solution.py:253
  108.0 14.5 %shard_map.165 = (f32[2,4,1,64,128]{4,3,2,1,0:T(8,128)S(1)}, f32[128,128]{1,0:T(8,128)S(1)}) custom-call(f32[2,4,1,64,128]{4,3,2,1,0:T(8,128)S(1)} %bitcast.70, f32[128,128]{1,0:T(8,128)S(1)} %maximum_maximum_fusion.gram_ref), custom_call_target="tpu_custom_call" | custom-call | tf_op jit(solution)/shard_map/pallas_call | solution.py:320
  123.4 3.2 %fusion.7 = (bf16[1,512,2560]{2,1,0:T(8,128)(2,1)}, bf16[512,2560]{1,0:T(8,128)(2,1)}) fusion(f32[512,2560]{1,0:T(8,128)S(1)} %convert_add_fusion, bf16[2560,128]{0,1:T(8,128)(2,1)S(1)} %convolution_convert_fusion.1, bf16[512,128]{0,1:T(8,128)(2,1)S(1)} %get-tuple-element.22), kind=kOutput, calls=%fused_computation.19 | convolution fusion | flops 171704320 | bytes 10878976 | tf_op jit(solution)/shard_map/dot_general | solution.py:441
  126.6 3.2 %fusion.6 = (bf16[1,2560,512]{2,1,0:T(8,128)(2,1)}, bf16[2560,512]{1,0:T(8,128)(2,1)}) fusion(f32[2560,512]{1,0:T(8,128)S(1)} %convert_add_fusion.1, bf16[512,128]{0,1:T(8,128)(2,1)S(1)} %get-tuple-element.22, bf16[2560,128]{0,1:T(8,128)(2,1)S(1)} %convolution_convert_fusion.1), kind=kOutput, calls=%fused_computation.18 | convolution fusion | flops 171704320 | bytes 10878976 | tf_op jit(solution)/shard_map/dot_general | solution.py:435
  (40 shorter events, 10.2 us)
Async XLA Ops:
  7.2 34.0 %copy-start = (bf16[2560,512]{1,0:T(8,128)(2,1)S(1)}, bf16[2560,512]{1,0:T(8,128)(2,1)}, u32[]{:S(2)}) copy-start(bf16[2560,512]{1,0:T(8,128)(2,1)} %param.18) | copy-start | bytes 7864324
  7.2 61.9 %all-gather.2.cloned.1.call-start = ((), (), s32[]{:S(2)}) async-start(), calls=%async_computation | async-start | bytes 3276800 | tf_op jit(solution)/shard_map/all_gather | solution.py:358
  11.2 1.0 copy-start.2
  32.6 1.3 copy-start.1
  33.9 4.2 %copy-start.11 = (s32[1,512]{1,0:T(1,128)S(1)}, s32[1,512]{1,0:T(1,128)}, u32[]{:S(2)}) copy-start(s32[1,512]{1,0:T(1,128)} %param.12) | copy-start | bytes 6148
  38.1 2.2 %copy-start.5 = (bf16[1,8,512,512]{3,2,1,0:T(8,128)(2,1)S(1)}, bf16[1,8,512,512]{3,2,1,0:T(8,128)(2,1)}, u32[]{:S(2)}) copy-start(bf16[1,8,512,512]{3,2,1,0:T(8,128)(2,1)} %param.16) | copy-start | bytes 12582916
  40.3 2.5 %copy-start.7 = (bf16[512,2560]{1,0:T(8,128)(2,1)}, bf16[512,2560]{1,0:T(8,128)(2,1)S(1)}, u32[]{:S(2)}) copy-start(bf16[512,2560]{1,0:T(8,128)(2,1)S(1)} %convolution_convert_fusion) | copy-start | bytes 7864324
  47.2 1.9 %copy-start.3 = (bf16[8,512,512]{2,1,0:T(8,128)(2,1)}, bf16[8,512,512]{2,1,0:T(8,128)(2,1)S(1)}, u32[]{:S(2)}) copy-start(bf16[8,512,512]{2,1,0:T(8,128)(2,1)S(1)} %fusion.2) | copy-start | bytes 12582916
  69.1 4.3 %copy-start.4 = (bf16[8,512,512]{2,1,0:T(8,128)(2,1)S(1)}, bf16[8,512,512]{2,1,0:T(8,128)(2,1)}, u32[]{:S(2)}) copy-start(bf16[8,512,512]{2,1,0:T(8,128)(2,1)} %copy-done.3) | copy-start | bytes 12582916
  73.4 1.7 %copy-start.6 = (bf16[1,2560,512]{2,1,0:T(8,128)(2,1)S(1)}, bf16[1,2560,512]{2,1,0:T(8,128)(2,1)}, u32[]{:S(2)}) copy-start(bf16[1,2560,512]{2,1,0:T(8,128)(2,1)} %param.20) | copy-start | bytes 7864324
  73.4 2.5 %copy-start.8 = (bf16[512,2560]{1,0:T(8,128)(2,1)S(1)}, bf16[512,2560]{1,0:T(8,128)(2,1)}, u32[]{:S(2)}) copy-start(bf16[512,2560]{1,0:T(8,128)(2,1)} %copy-done.7) | copy-start | bytes 7864324
  77.5 1.7 %copy-start.9 = (bf16[1,512,2560]{2,1,0:T(8,128)(2,1)S(1)}, bf16[1,512,2560]{2,1,0:T(8,128)(2,1)}, u32[]{:S(2)}) copy-start(bf16[1,512,2560]{2,1,0:T(8,128)(2,1)} %param.21) | copy-start | bytes 7864324
  77.5 2.5 %copy-start.10 = (bf16[1,512,2560]{2,1,0:T(8,128)(2,1)S(1)}, bf16[1,512,2560]{2,1,0:T(8,128)(2,1)}, u32[]{:S(2)}) copy-start(bf16[1,512,2560]{2,1,0:T(8,128)(2,1)} %all-gather.2.cloned.1.call-done) | copy-start | bytes 7864324
Sparse Core Ops, SparseCore 0:
  9.6 59.3 all-gather.1

commit v5 on v4

--- a/solution.py
+++ b/solution.py
@@ -45,7 +45,7 @@
     pl.semaphore_wait(barrier, len(peers))
 
 
-def table_kernel(chips, depth, rows_ref, gain_ref, out_ref, gout_ref, sz, rz, sg, rg, sp, rp, sc, rc, local):
+def table_kernel(chips, depth, rows_ref, gain_ref, dy_ref, out_ref, gout_ref, dout_ref, sz, rz, sg, rg, sp, rp, sc, rc, sd, rd, local):
     me, core, chip, z = position(chips, depth)
     sibling = chip * 2 + 1 - core
     width = rows_ref.shape[2]
@@ -59,6 +59,10 @@
     own.start()
     own_gain = pltpu.make_async_copy(gain_ref, gout_ref.at[z], local.at[1])
     own_gain.start()
+    own_dy = pltpu.make_async_copy(
+        dy_ref, dout_ref.at[:, pl.ds(pl.multiple_of(z * width, 128), width)], local.at[2]
+    )
+    own_dy.start()
     greet(chips, depth)
     sends = []
     along = {}
@@ -71,6 +75,18 @@
         along[j] = (copy, gain)
         sends += [copy, gain]
     waits = []
+    for j in range(1, depth):
+        copy = remote(
+            dy_ref,
+            dout_ref.at[:, pl.ds(pl.multiple_of(z * width, 128), width)],
+            sd.at[j],
+            rd.at[j],
+            me,
+            lax.rem(z + j, depth),
+        )
+        copy.start()
+        waits.append(copy)
+        sends.append(copy)
     plane = {}
     for j in range(1, depth):
         along[j][0].wait_recv()
@@ -98,6 +114,7 @@
             sends.append(copy)
     own.wait()
     own_gain.wait()
+    own_dy.wait()
     for j in range(1, depth):
         along[j][1].wait_recv()
     for copy in waits:
@@ -106,7 +123,7 @@
         copy.wait_send()
 
 
-def gather_table(embedding, norm_gain, replicas, depth):
+def gather_table(embedding, norm_gain, dy_part, replicas, depth):
     chips = replicas // 2
     vocab, width = embedding.shape
     rows = embedding.reshape(replicas, vocab // replicas, width)
@@ -114,11 +131,12 @@
     whole = jax.ShapeDtypeStruct(rows.shape[:2] + (depth * width,), rows.dtype)
     gains = jax.ShapeDtypeStruct((depth, 16, width), gain.dtype)
     sem = pltpu.SemaphoreType.DMA
-    table, gains = pl.pallas_call(
+    dy_all = jax.ShapeDtypeStruct((dy_part.shape[0], depth * width), dy_part.dtype)
+    table, gains, dy_part = pl.pallas_call(
         functools.partial(table_kernel, chips, depth),
-        out_shape=(whole, gains),
-        in_specs=[pl.BlockSpec(memory_space=pltpu.VMEM)] * 2,
-        out_specs=[pl.BlockSpec(memory_space=pltpu.VMEM)] * 2,
+        out_shape=(whole, gains, dy_all),
+        in_specs=[pl.BlockSpec(memory_space=pltpu.VMEM)] * 3,
+        out_specs=[pl.BlockSpec(memory_space=pltpu.VMEM)] * 3,
         scratch_shapes=[
             sem((depth,)),
             sem((depth,)),
@@ -128,14 +146,16 @@
             sem((chips, depth)),
             sem((chips, depth)),
             sem((chips, depth)),
-            sem((2,)),
+            sem((depth,)),
+            sem((depth,)),
+            sem((3,)),
         ],
         compiler_params=pltpu.CompilerParams(
             collective_id=0, has_side_effects=True, vmem_limit_bytes=VMEM_LIMIT
         ),
-    )(rows, gain)
+    )(rows, gain, dy_part)
     table = table.reshape(vocab, depth * width)
-    return table, gains[:, 0, :].reshape(depth * width)
+    return table, gains[:, 0, :].reshape(depth * width), dy_part
 
 
 def reduce_steps(chips, depth, p_ref, out_ref, b1, b2, b3, sems, between):
@@ -355,9 +375,11 @@
     vocab = embedding.shape[0]
     rows = samples * seq
     rank = q_value.shape[1]
-    dy_whole = lax.all_gather(cotangent, "mdl", axis=2, tiled=True)
-    width_full = dy_whole.shape[2]
-    raw, gain = gather_table(embedding, norm_gain, replicas, depth)
+    flat_dy = cotangent.reshape(rows, -1)
+    held = rows - rows // 4
+    dy_most = lax.all_gather(flat_dy[:held], "mdl", axis=1, tiled=True)
+    width_full = dy_most.shape[1]
+    raw, gain, dy_rest = gather_table(embedding, norm_gain, flat_dy[held:], replicas, depth)
     raw = raw.astype(jnp.float32)
     scale = lax.rsqrt(jnp.sum(raw * raw, axis=1) / width_full + 1e-06)
     table = (raw * scale[:, None] * gain.astype(jnp.float32)[None, :]).astype(jnp.bfloat16)
@@ -379,9 +401,8 @@
         .astype(jnp.bfloat16)
         .reshape(rows, inner_local)
     )
-    dy_rows = jnp.where(live[..., None], dy_whole, jnp.zeros_like(dy_whole)).reshape(
-        rows, width_full
-    )
+    dy_whole = jnp.concatenate([dy_most, dy_rest], axis=0)
+    dy_rows = jnp.where(live.reshape(rows, 1), dy_whole, jnp.zeros_like(dy_whole))
     dcontext = lax.dot_general(
         dy_rows, w_out, (((1,), (1,)), ((), ())), preferred_element_type=jnp.float32
     ).astype(jnp.bfloat16)

time: 138 us -> 152 us (1.10)
  Pallas kernels: 58 us -> 88.5 us
  waiting for transfers between devices: 19.2 us -> 0.02 us
  local copies, waits for them, and re-layouts: 9.83 us -> 12 us
    pallas_call x1, Pallas kernels: 20.4 us -> 43.1 us  [gather_table(): pl.pallas_call(functools.partial(table_kernel, chips, depth), out_shape=(...]
    all_gather x1, waiting for transfers between devices: 18.5 us -> 0.01 us  [shards(): dy_most = lax.all_gather(flat_dy[:held], 'mdl', axis=1, tiled=True)]
    pallas_call x1, Pallas kernels: 23.1 us -> 31.3 us  [reduce_left(): pl.pallas_call(functools.partial(left_kernel, chips, depth), out_shape=ja...]
    slice x0 -> x2, local copies, waits for them, and re-layouts: none -> 2.94 us  [the longest x1 2 us: shards(): dy_most = lax.all_gather(flat_dy[:held], 'mdl', axis=1, tiled=True)]
    unnamed x24 -> x26, local copies, waits for them, and re-layouts: 8.26 us -> 7.48 us
  transfers between devices with their start and end apart: 1 -> 1, of which waited for: 1 -> 0; matrix products, arithmetic and copies ran while one was open for 12% -> 12% of each run, Pallas kernels for 15% -> 28%
where the time goes in v5:
time: 152 us; the launch traced here: 151 us
  Pallas kernels  88.5 us (58%)
  matrix products  24.5 us (16%)
  between operations  15 us (10%)
  local copies, waits for them, and re-layouts  12 us (8%)
  other arithmetic  11.4 us (8%)
    pallas_call x1, Pallas kernels, gather_table(): pl.pallas_call(functools.partial(table_kernel, chips, depth), out_shape=(...  43.1 us
    pallas_call x1, Pallas kernels, reduce_left(): pl.pallas_call(functools.partial(left_kernel, chips, depth), out_shape=ja...  31.3 us
    pallas_call x1, Pallas kernels, reduce_right(): pl.pallas_call(functools.partial(right_kernel, chips, rank), out_shape=(j...  14.1 us
    unnamed x26, local copies, waits for them, and re-layouts  7.48 us
    another operation x3, other arithmetic  4.13 us
    dot_general x1, matrix products, shards(): lax.dot_general(dy_rows, w_out, (((1,), (1,)), ((), ())), preferred_eleme...  4.1 us
    dot_general x1, matrix products, shards(): lax.dot_general(rough_phat[:, :rank], rough_q[:, :rank], (((1,), (1,)), (...  3.22 us
    dot_general x1, matrix products, shards(): lax.dot_general(rough_q[:, rank:], rough_phat[:, rank:], (((1,), (1,)), (...  3.22 us
  transfers between devices with their start and end apart: 1, of which 0 were waited for; matrix products, arithmetic and copies ran while one was open for 12% of the time, Pallas kernels for 28%

profile of v5, /device:TPU:0, one launch (start us, length us, event | category | flops | bytes accessed | tf_op | source)
XLA Modules:
  0.0 151.4 jit_solution(1016157320522679471)
XLA Ops:
  7.2 2.0 %slice.42 = bf16[1,384,640]{2,1,0:T(8,128)(2,1)} slice(bf16[1,512,640]{2,1,0:T(8,128)(2,1)} %param.17), slice={[0:1], [0:384], [0:640]} | slice | bytes 983040 | tf_op jit(solution)/shard_map/slice | solution.py:380
  9.3 0.9 slice_bitcast_fusion.dy_ref
  10.9 0.9 convert.12
  11.8 0.9 convert.13
  13.4 1.0 copy-done.2
  14.4 43.1 %shard_map.163 = (bf16[8,48,2560]{2,1,0:T(8,128)(2,1)S(1)}, bf16[4,16,640]{2,1,0:T(8,128)(2,1)S(1)}, bf16[128,2560]{1,0:T(8,128)(2,1)S(1)}) custom-call(bf16[8,48,640]{2,1,0:T(8,128)(2,1)S(1)} %bitcast.67, bf16[16,640]{1,0:T(8,128)(2,1)S(1)} %broadcast_in_dim.61.gain_ref, bf16[128,640]{1,0:T(8,128)(2,1)S(1)} %slice_bitcast_fusion.dy_ref), custom_call_target="tpu_custom_call" | custom-call | tf_op jit(solution)/shard_map/pallas_call | solution.py:135
  57.5 1.3 copy-done.1
  58.9 2.0 %multiply_reduce_fusion = f32[8,48]{1,0:T(8,128)S(1)} fusion(bf16[8,48,2560]{2,1,0:T(8,128)(2,1)} %copy-done.1), kind=kLoop, calls=%fused_computation.14 | loop fusion | flops 2948736 | bytes 1967616 | tf_op jit(solution)/shard_map/reduce_sum | solution.py:384
  61.0 2.1 %fusion.4 = bf16[384,2560]{1,0:T(8,128)(2,1)S(1)} fusion(f32[2560]{0:T(1024)S(1)} %reshape.126, f32[384]{0:T(512)S(1)} %rsqrt.11, bf16[8,48,2560]{2,1,0:T(8,128)(2,1)} %copy-done.1), kind=kLoop, calls=%fused_computation.13 | loop fusion | flops 3932160 | bytes 3943936 | tf_op jit(solution)/shard_map/convert_element_type | solution.py:385
  63.1 1.6 %convolution_convert_fusion = bf16[512,2560]{1,0:T(8,128)(2,1)S(1)} fusion(bf16[384,2560]{1,0:T(8,128)(2,1)S(1)} %fusion.4, s32[512]{0:T(512)S(1)} %bitcast.75), kind=kOutput, calls=%fused_computation.9 | convolution fusion | flops 1008140288 | bytes 4589568 | tf_op jit(solution)/shard_map/dot_general | solution.py:388
  65.3 0.9 fusion
  66.2 1.6 %convolution_convert_fusion.4 = bf16[512,512]{0,1:T(8,128)(2,1)S(1)} fusion(bf16[512,2560]{1,0:T(8,128)(2,1)S(1)} %convolution_convert_fusion, bf16[2560,512]{1,0:T(8,128)(2,1)S(1)} %copy-done), kind=kOutput, calls=%fused_computation.30 | convolution fusion | flops 1342439424 | bytes 5767168 | tf_op jit(solution)/shard_map/dot_general | solution.py:393
  67.7 2.1 %fusion.1 = f32[8,512]{1,0:T(8,128)S(1)} fusion(bf16[1,8,512,512]{3,2,1,0:T(8,128)(2,1)S(1)} %copy-done.5, f32[8,512]{1,0:T(8,128)S(1)} %fusion, pred[512]{0:T(512)(128)(4,1)S(1)} %iota_compare_fusion.3), kind=kLoop, calls=%fused_computation.4 | loop fusion | flops 8384512 | bytes 4227584 | tf_op jit(solution)/shard_map/reduce_sum | solution.py:397
  69.9 2.3 %fusion.2 = bf16[8,512,512]{2,1,0:T(8,128)(2,1)S(1)} fusion(bf16[1,8,512,512]{3,2,1,0:T(8,128)(2,1)S(1)} %copy-done.5, f32[8,512]{1,0:T(8,128)S(1)} %fusion.1, f32[8,512]{1,0:T(8,128)S(1)} %fusion, pred[512]{0:T(512)(128)(4,1)S(1)} %iota_compare_fusion.3), kind=kLoop, calls=%fused_computation.10 | loop fusion | flops 10485760 | bytes 8421888 | tf_op jit(solution)/shard_map/reshape.7
  72.2 1.9 %copy-done.3 = bf16[8,512,512]{2,1,0:T(8,128)(2,1)} copy-done((bf16[8,512,512]{2,1,0:T(8,128)(2,1)}, bf16[8,512,512]{2,1,0:T(8,128)(2,1)S(1)}, u32[]{:S(2)}) %copy-start.3) | copy-done | bytes 4194328
  74.1 2.2 %convolution_convert_fusion.2 = bf16[8,64,512]{2,1,0:T(8,128)(2,1)} fusion(bf16[512,8,64]{0,2,1:T(8,128)(2,1)S(1)} %bitcast.71, bf16[8,512,512]{2,1,0:T(8,128)(2,1)S(1)} %fusion.2), kind=kOutput, calls=%fused_computation.28 | convolution fusion | flops 268697600 | bytes 5242880 | tf_op jit(solution)/shard_map/shqk,skhd->sqhd/dot_general | solution.py:400
  76.3 4.1 %convolution_convert_fusion.5 = bf16[512,512]{0,1:T(8,128)(2,1)S(1)} fusion(bf16[512,2560]{1,0:T(8,128)(2,1)} %param.19, bf16[128,2560]{1,0:T(8,128)(2,1)S(1)} %get-tuple-element.13, bf16[384,2560]{1,0:T(8,128)(2,1)} %bitcast.73, pred[512]{0:T(512)(128)(4,1)S(1)} %iota_compare_fusion.3), kind=kOutput, calls=%fused_computation.31 | convolution fusion | flops 1348993024 | bytes 5767680 | tf_op jit(solution)/shard_map/dot_general | solution.py:406
  82.9 1.6 %convert_add_fusion = f32[512,2560]{1,0:T(8,128)S(1)} fusion(bf16[512,512]{0,1:T(8,128)(2,1)S(1)} %bitcast.70, bf16[1,512,2560]{2,1,0:T(8,128)(2,1)S(1)} %copy-done.10, bf16[128,2560]{1,0:T(8,128)(2,1)S(1)} %get-tuple-element.13, bf16[384,2560]{1,0:T(8,128)(2,1)S(1)} %bitcast.74, pred[512]{0:T(512)(128)(4,1)S(1)} %iota_compare_fusion.3), kind=kOutput, calls=%fused_computation.5 | convolution fusion | flops 1351352320 | bytes 11010560 | tf_op jit(solution)/shard_map/dot_general | solution.py:415
  85.5 1.6 %convert_add_fusion.1 = f32[2560,512]{1,0:T(8,128)S(1)} fusion(bf16[512,2560]{1,0:T(8,128)(2,1)S(1)} %copy-done.8, bf16[512,512]{0,1:T(8,128)(2,1)S(1)} %bitcast.69, bf16[1,2560,512]{2,1,0:T(8,128)(2,1)S(1)} %copy-done.6), kind=kOutput, calls=%fused_computation.6 | convolution fusion | flops 1344798720 | bytes 11010048 | tf_op jit(solution)/shard_map/dot_general | solution.py:418
  87.9 0.9 fusion.5
  88.8 31.3 %shard_map.164 = bf16[2,4,4,80,128]{4,3,2,1,0:T(8,128)(2,1)S(1)} custom-call(bf16[2,4,4,80,128]{4,3,2,1,0:T(8,128)(2,1)S(1)} %bitcast.65), custom_call_target="tpu_custom_call" | custom-call | tf_op jit(solution)/shard_map/pallas_call | solution.py:273
  122.4 14.1 %shard_map.165 = (f32[2,4,1,64,128]{4,3,2,1,0:T(8,128)S(1)}, f32[128,128]{1,0:T(8,128)S(1)}) custom-call(f32[2,4,1,64,128]{4,3,2,1,0:T(8,128)S(1)} %bitcast.66, f32[128,128]{1,0:T(8,128)S(1)} %maximum_maximum_fusion.gram_ref), custom_call_target="tpu_custom_call" | custom-call | tf_op jit(solution)/shard_map/pallas_call | solution.py:340
  137.4 3.2 %fusion.7 = (bf16[1,512,2560]{2,1,0:T(8,128)(2,1)}, bf16[512,2560]{1,0:T(8,128)(2,1)}) fusion(f32[512,2560]{1,0:T(8,128)S(1)} %convert_add_fusion, bf16[2560,128]{0,1:T(8,128)(2,1)S(1)} %convolution_convert_fusion.1, bf16[512,128]{0,1:T(8,128)(2,1)S(1)} %get-tuple-element.24), kind=kOutput, calls=%fused_computation.19 | convolution fusion | flops 171704320 | bytes 10878976 | tf_op jit(solution)/shard_map/dot_general | solution.py:462
  140.6 3.2 %fusion.6 = (bf16[1,2560,512]{2,1,0:T(8,128)(2,1)}, bf16[2560,512]{1,0:T(8,128)(2,1)}) fusion(f32[2560,512]{1,0:T(8,128)S(1)} %convert_add_fusion.1, bf16[512,128]{0,1:T(8,128)(2,1)S(1)} %get-tuple-element.24, bf16[2560,128]{0,1:T(8,128)(2,1)S(1)} %convolution_convert_fusion.1), kind=kOutput, calls=%fused_computation.18 | convolution fusion | flops 171704320 | bytes 10878976 | tf_op jit(solution)/shard_map/dot_general | solution.py:456
  (44 shorter events, 9.7 us)
Async XLA Ops:
  7.2 59.0 %copy-start = (bf16[2560,512]{1,0:T(8,128)(2,1)S(1)}, bf16[2560,512]{1,0:T(8,128)(2,1)}, u32[]{:S(2)}) copy-start(bf16[2560,512]{1,0:T(8,128)(2,1)} %param.18) | copy-start | bytes 7864324
  7.2 69.1 %all-gather.3.cloned.1.call-start = ((), (), s32[]{:S(2)}) async-start(), calls=%async_computation | async-start | bytes 2457600 | tf_op jit(solution)/shard_map/all_gather | solution.py:380
  13.4 1.0 copy-start.2
  57.5 1.3 copy-start.1
  58.9 4.2 %copy-start.12 = (s32[1,512]{1,0:T(1,128)S(1)}, s32[1,512]{1,0:T(1,128)}, u32[]{:S(2)}) copy-start(s32[1,512]{1,0:T(1,128)} %param.12) | copy-start | bytes 6148
  63.1 2.2 %copy-start.5 = (bf16[1,8,512,512]{3,2,1,0:T(8,128)(2,1)S(1)}, bf16[1,8,512,512]{3,2,1,0:T(8,128)(2,1)}, u32[]{:S(2)}) copy-start(bf16[1,8,512,512]{3,2,1,0:T(8,128)(2,1)} %param.16) | copy-start | bytes 12582916
  65.2 2.5 %copy-start.7 = (bf16[512,2560]{1,0:T(8,128)(2,1)}, bf16[512,2560]{1,0:T(8,128)(2,1)S(1)}, u32[]{:S(2)}) copy-start(bf16[512,2560]{1,0:T(8,128)(2,1)S(1)} %convolution_convert_fusion) | copy-start | bytes 7864324
  72.2 2.0 %copy-start.3 = (bf16[8,512,512]{2,1,0:T(8,128)(2,1)}, bf16[8,512,512]{2,1,0:T(8,128)(2,1)S(1)}, u32[]{:S(2)}) copy-start(bf16[8,512,512]{2,1,0:T(8,128)(2,1)S(1)} %fusion.2) | copy-start | bytes 12582916
  76.3 4.1 %copy-start.4 = (bf16[8,512,512]{2,1,0:T(8,128)(2,1)S(1)}, bf16[8,512,512]{2,1,0:T(8,128)(2,1)}, u32[]{:S(2)}) copy-start(bf16[8,512,512]{2,1,0:T(8,128)(2,1)} %copy-done.3) | copy-start | bytes 12582916
  80.4 1.0 copy-start.9
  80.4 1.9 %copy-start.10 = (bf16[1,512,2560]{2,1,0:T(8,128)(2,1)S(1)}, bf16[1,512,2560]{2,1,0:T(8,128)(2,1)}, u32[]{:S(2)}) copy-start(bf16[1,512,2560]{2,1,0:T(8,128)(2,1)} %param.21) | copy-start | bytes 7864324
  80.4 2.5 %copy-start.11 = (bf16[1,384,2560]{2,1,0:T(8,128)(2,1)S(1)}, bf16[1,384,2560]{2,1,0:T(8,128)(2,1)}, u32[]{:S(2)}) copy-start(bf16[1,384,2560]{2,1,0:T(8,128)(2,1)} %all-gather.3.cloned.1.call-done) | copy-start | bytes 5898244
  82.9 1.7 %copy-start.6 = (bf16[1,2560,512]{2,1,0:T(8,128)(2,1)S(1)}, bf16[1,2560,512]{2,1,0:T(8,128)(2,1)}, u32[]{:S(2)}) copy-start(bf16[1,2560,512]{2,1,0:T(8,128)(2,1)} %param.20) | copy-start | bytes 7864324
  82.9 2.5 %copy-start.8 = (bf16[512,2560]{1,0:T(8,128)(2,1)S(1)}, bf16[512,2560]{1,0:T(8,128)(2,1)}, u32[]{:S(2)}) copy-start(bf16[512,2560]{1,0:T(8,128)(2,1)} %copy-done.7) | copy-start | bytes 7864324
Sparse Core Ops, SparseCore 0:
  10.2 64.2 all-gather.2
